TPU v7x, 512 devices: a whole 4x8x8 slice. The times are simulated.
512 devices in a mesh: seq: 64 (over x, z_hi, y), chan: 8 (over z_lo, core).
Axes of the slice: x: 4, y: 8, z: 8 (z_hi: 2, z_lo: 4; z = z_hi * 4 + z_lo), core: 2. Of those that a mesh axis runs over, the one named last changes fastest.
Arguments:
- values: bfloat16 [8192, 8192], P('seq', 'chan'), may hold values from -6 to 6
- gate: bfloat16 [8192, 8192], P('seq', 'chan'), may hold values from -6 to 6
- skip: float32 [8192], P('chan'), may hold values from 0.5 to 1.5
- spectrum: float32 [2, 128, 128, 8192], P(None, 'seq', None, 'chan'), may hold values from -8 to 8
- out_weight: bfloat16 [4096, 8192], P('seq', 'chan'), may hold values from -0.0625 to 0.0625
Outputs:
- result: bfloat16 [8192, 4096], P('seq', 'chan')
All inputs are finite; a program needn't handle non-finite values.
Results may differ from a plain program's by a relative error of at most 0.0049.
Values may be sent and summed in bfloat16 or wider, within the bound.
A program may use at most 64 MiB of HBM per device.

v0:
```python
import math

import jax
import jax.numpy as jnp
from jax import lax
from jax.sharding import PartitionSpec as P

high = lax.Precision.HIGHEST


def angle_table(rows, cols, period):
    product = (
        jnp.arange(rows, dtype=jnp.int32)[:, None]
        * jnp.arange(cols, dtype=jnp.int32)[None, :]
        % period
    )
    theta = product.astype(jnp.float32) * (2.0 * math.pi / period)
    return (jnp.cos(theta), jnp.sin(theta))


def spectral_core(freq_re, freq_im, spec_re, spec_im, cos_hr, sin_hr):
    f_re = jnp.einsum("hr,grc->ghc", cos_hr, freq_re, precision=high) + jnp.einsum(
        "hr,grc->ghc", sin_hr, freq_im, precision=high
    )
    f_im = jnp.einsum("hr,grc->ghc", cos_hr, freq_im, precision=high) - jnp.einsum(
        "hr,grc->ghc", sin_hr, freq_re, precision=high
    )
    prod_re = f_re * spec_re - f_im * spec_im
    prod_im = f_re * spec_im + f_im * spec_re
    back_re = jnp.einsum("rh,ghc->grc", cos_hr, prod_re, precision=high) - jnp.einsum(
        "rh,ghc->grc", sin_hr, prod_im, precision=high
    )
    back_im = jnp.einsum("rh,ghc->grc", cos_hr, prod_im, precision=high) + jnp.einsum(
        "rh,ghc->grc", sin_hr, prod_re, precision=high
    )
    return (back_re, back_im)


def body(values, gate, skip, spectrum, out_weight):
    parts = lax.axis_size("seq")
    me_seq = lax.axis_index("seq")
    tok, chans = values.shape
    groups = 2 * parts
    total = groups * tok
    cos_ga, sin_ga = angle_table(groups, parts, groups)
    cos_hr, sin_hr = angle_table(tok, tok, tok)
    reach = tok // parts
    offsets = me_seq * reach + jnp.arange(reach, dtype=jnp.int32)
    twist = jnp.arange(groups, dtype=jnp.int32)[:, None] * offsets[None, :] % total
    twist = twist.astype(jnp.float32) * (2.0 * math.pi / total)
    cos_tw = jnp.cos(twist)[:, :, None]
    sin_tw = jnp.sin(twist)[:, :, None]
    moved, gate_moved = (
        lax.all_to_all(
            values.reshape(parts, reach, chans), "seq", split_axis=0, concat_axis=0, tiled=True
        ),
        lax.all_to_all(
            gate.reshape(parts, reach, chans), "seq", split_axis=0, concat_axis=0, tiled=True
        ),
    )
    stream = moved.astype(jnp.float32)
    part_re = jnp.einsum("ga,arc->grc", cos_ga, stream, precision=high)
    part_im = -jnp.einsum("ga,arc->grc", sin_ga, stream, precision=high)
    turned_re = part_re * cos_tw + part_im * sin_tw
    turned_im = part_im * cos_tw - part_re * sin_tw
    freq = lax.all_to_all(
        jnp.stack([turned_re, turned_im]), "seq", split_axis=1, concat_axis=2, tiled=True
    )
    back_re, back_im = spectral_core(freq[0], freq[1], spectrum[0], spectrum[1], cos_hr, sin_hr)
    spread = lax.all_to_all(
        jnp.stack([back_re, back_im]), "seq", split_axis=2, concat_axis=1, tiled=True
    )
    untwist_re = spread[0] * cos_tw - spread[1] * sin_tw
    untwist_im = spread[1] * cos_tw + spread[0] * sin_tw
    conv_part = (
        jnp.einsum("ga,grc->arc", cos_ga, untwist_re, precision=high)
        - jnp.einsum("ga,grc->arc", sin_ga, untwist_im, precision=high)
    ) * (1.0 / total)
    mixed = (gate_moved.astype(jnp.float32) * (conv_part + skip * stream)).astype(jnp.bfloat16)
    mixed = mixed.reshape(parts * reach, chans)
    partial_out = lax.dot_general(
        mixed,
        lax.all_gather(out_weight, "seq", axis=0, tiled=True),
        (((1,), (1,)), ((), ())),
        preferred_element_type=jnp.float32,
    )
    summed = lax.psum_scatter(partial_out, "chan", scatter_dimension=1, tiled=True).astype(
        jnp.bfloat16
    )
    shaped = summed.reshape(parts, tok // parts, summed.shape[1])
    returned = lax.all_to_all(shaped, "seq", split_axis=0, concat_axis=1, tiled=True)
    return returned.reshape(tok, summed.shape[1])


def solution(mesh):
    placed = (
        P("seq", "chan"),
        P("seq", "chan"),
        P("chan"),
        P(None, "seq", None, "chan"),
        P("seq", "chan"),
    )
    return jax.shard_map(
        body, mesh=mesh, in_specs=placed, out_specs=P("seq", "chan"), check_vma=False
    )
```

profile of v0, /device:TPU:6, one launch (start us, length us, event | category | flops | bytes accessed | tf_op | source)
XLA Modules:
  0.0 363.3 jit_solution(11590143543225215303)
XLA Ops:
  6.5 0.7 all-gather.2.cloned.1.call-update
  7.3 1.8 reshape.84
  9.0 19.2 %all-to-all-start.1 = ((bf16[64,2,1024]{2,1,0:T(2,128)(2,1)}), bf16[64,2,1024]{2,1,0:T(2,128)(2,1)S(1)}, u32[]{:S(2)}, u32[]{:S(2)}) async-start(bf16[64,2,1024]{2,1,0:T(2,128)(2,1)} %reshape.84), calls=%async_computation.1 | async-start | bytes 524288 | tf_op jit(solution)/shard_map/all_to_all | solution.py:54
  28.3 0.1 fusion.72
  28.4 15.1 %all-to-all-done.1 = bf16[64,2,1024]{2,1,0:T(2,128)(2,1)S(1)} async-done(((bf16[64,2,1024]{2,1,0:T(2,128)(2,1)}), bf16[64,2,1024]{2,1,0:T(2,128)(2,1)S(1)}, u32[]{:S(2)}, u32[]{:S(2)}) %all-to-all-start.1) | async-done | bytes 262176 | tf_op jit(solution)/shard_map/all_to_all | solution.py:54
  43.5 0.7 convolution_negate_fusion
  44.3 1.0 add_bitcast_fusion
  45.3 0.2 pad_maximum_fusion
  45.5 3.0 copy.27
  48.5 6.9 %all-to-all-start.2 = ((f32[2,128,2,1024]{3,2,0,1:T(2,128)}), f32[2,128,2,1024]{3,2,0,1:T(2,128)S(1)}, u32[]{:S(2)}, u32[]{:S(2)}) async-start(f32[2,128,2,1024]{3,2,0,1:T(2,128)} %copy.27), calls=%async_computation.2 | async-start | bytes 4194304 | tf_op jit(solution)/shard_map/all_to_all | solution.py:66
  55.5 3.1 fusion.122
  58.6 1.5 copy.41
  60.2 2.5 copy.42
  62.7 48.0 %all-to-all-done.2 = f32[2,128,2,1024]{3,2,0,1:T(2,128)S(1)} async-done(((f32[2,128,2,1024]{3,2,0,1:T(2,128)}), f32[2,128,2,1024]{3,2,0,1:T(2,128)S(1)}, u32[]{:S(2)}, u32[]{:S(2)}) %all-to-all-start.2) | async-done | bytes 2097184 | tf_op jit(solution)/shard_map/all_to_all | solution.py:66
  110.7 1.6 copy.52
  112.3 1.9 fusion.123
  114.2 0.5 copy.29
  114.7 1.7 copy.30
  116.4 1.2 fusion.37
  117.6 1.2 fusion.35
  118.8 1.2 fusion.3
  120.1 1.5 fusion.8
  121.6 1.2 fusion.33
  122.8 1.2 fusion.1
  124.1 1.2 fusion.31
  125.3 1.2 fusion
  126.5 0.1 pad_maximum_fusion.1
  126.7 2.5 copy.35
  129.1 9.4 %all-to-all-start.3 = ((f32[2,2,128,1024]{3,1,0,2:T(2,128)}), f32[2,2,128,1024]{3,1,0,2:T(2,128)S(1)}, u32[]{:S(2)}, u32[]{:S(2)}) async-start(f32[2,2,128,1024]{3,1,0,2:T(2,128)} %copy.35), calls=%async_computation.3 | async-start | bytes 4194304 | tf_op jit(solution)/shard_map/all_to_all | solution.py:70
  138.6 0.8 reshape.83
  139.4 54.3 %all-to-all-done.3 = f32[2,2,128,1024]{3,1,0,2:T(2,128)S(1)} async-done(((f32[2,2,128,1024]{3,1,0,2:T(2,128)}), f32[2,2,128,1024]{3,1,0,2:T(2,128)S(1)}, u32[]{:S(2)}, u32[]{:S(2)}) %all-to-all-start.3) | async-done | bytes 2097184 | tf_op jit(solution)/shard_map/all_to_all | solution.py:70
  193.6 10.3 %all-to-all-start = ((bf16[64,2,1024]{2,1,0:T(2,128)(2,1)}), bf16[64,2,1024]{2,1,0:T(2,128)(2,1)}, u32[]{:S(2)}, u32[]{:S(2)}) async-start(bf16[64,2,1024]{2,1,0:T(2,128)(2,1)} %reshape.83), calls=%async_computation | async-start | bytes 524288 | tf_op jit(solution)/shard_map/all_to_all | solution.py:57
  204.0 0.8 copy.36
  204.8 1.9 fusion.121
  206.8 0.7 squeeze.24
  207.5 1.3 copy.38
  208.8 0.7 squeeze.25
  209.5 1.0 fusion.13
  210.5 7.9 %all-to-all-done = bf16[64,2,1024]{2,1,0:T(2,128)(2,1)} async-done(((bf16[64,2,1024]{2,1,0:T(2,128)(2,1)}), bf16[64,2,1024]{2,1,0:T(2,128)(2,1)}, u32[]{:S(2)}, u32[]{:S(2)}) %all-to-all-start) | async-done | bytes 262176 | tf_op jit(solution)/shard_map/all_to_all | solution.py:57
  218.4 2.1 fusion.7
  220.5 0.3 copy.40
  220.8 0.1 reshape.85
  220.9 59.7 %all-gather.2.cloned.1.call-done = bf16[4096,1024]{1,0:T(8,128)(2,1)} async-done(((bf16[64,1024]{1,0:T(8,128)(2,1)}), bf16[4096,1024]{1,0:T(8,128)(2,1)}) %all-gather.2.cloned.1.call-update) | async-done | bytes 8388624 | tf_op jit(solution)/shard_map/all_gather | solution.py:83
  280.6 7.6 %fusion.128 = f32[128,4096]{1,0:T(8,128)} fusion(bf16[128,1024]{1,0:T(8,128)(2,1)S(1)} %reshape.85, bf16[4096,1024]{1,0:T(8,128)(2,1)} %all-gather.2.cloned.1.call-done), kind=kOutput, calls=%fused_computation.137 | convolution fusion | flops 1073741824 | bytes 10747904 | tf_op jit(solution)/shard_map/dot_general | solution.py:81
  288.2 39.9 %reduce-scatter.2.cloned.1.call-done = f32[128,512]{1,0:T(8,128)} async-done(((f32[128,4096]{1,0:T(8,128)}), f32[128,512]{1,0:T(8,128)}) %reduce-scatter.2.cloned.1.call-update) | async-done | bytes 262160 | tf_op jit(solution)/shard_map/reduce_scatter | solution.py:87
  328.1 1.0 convert_element_type.54
  329.1 26.6 %all_to_all.49 = bf16[64,2,512]{2,1,0:T(2,128)(2,1)S(1)} all-to-all(bf16[64,2,512]{2,1,0:T(2,128)(2,1)S(1)} %reshape.86), channel_id=1, replica_groups=mesh['seq'=64,'chan'=8] {'seq'}, dimensions={0} | all-to-all | bytes 262144 | tf_op jit(solution)/shard_map/all_to_all | solution.py:91
  355.7 0.7 reshape.87
  (12 shorter events, 0.2 us)
Async XLA Ops:
  6.5 274.1 %all-gather.2.cloned.1.call-start = ((), (), s32[]{:S(2)}) async-start(), calls=%async_computation.6 | async-start | bytes 8519680 | tf_op jit(solution)/shard_map/all_gather | solution.py:83
  9.0 34.5 %all-to-all-start.1 = ((bf16[64,2,1024]{2,1,0:T(2,128)(2,1)}), bf16[64,2,1024]{2,1,0:T(2,128)(2,1)S(1)}, u32[]{:S(2)}, u32[]{:S(2)}) async-start(bf16[64,2,1024]{2,1,0:T(2,128)(2,1)} %reshape.84), calls=%async_computation.1 | async-start | bytes 524288 | tf_op jit(solution)/shard_map/all_to_all | solution.py:54
  48.5 62.1 %all-to-all-start.2 = ((f32[2,128,2,1024]{3,2,0,1:T(2,128)}), f32[2,128,2,1024]{3,2,0,1:T(2,128)S(1)}, u32[]{:S(2)}, u32[]{:S(2)}) async-start(f32[2,128,2,1024]{3,2,0,1:T(2,128)} %copy.27), calls=%async_computation.2 | async-start | bytes 4194304 | tf_op jit(solution)/shard_map/all_to_all | solution.py:66
  118.8 1.3 copy-start
  129.1 9.4 %copy-start.1 = (bf16[128,1024]{1,0:T(8,128)(2,1)S(1)}, bf16[128,1024]{1,0:T(8,128)(2,1)}, u32[]{:S(2)}) copy-start(bf16[128,1024]{1,0:T(8,128)(2,1)} %param.6) | copy-start | bytes 786436
  129.1 64.5 %all-to-all-start.3 = ((f32[2,2,128,1024]{3,1,0,2:T(2,128)}), f32[2,2,128,1024]{3,1,0,2:T(2,128)S(1)}, u32[]{:S(2)}, u32[]{:S(2)}) async-start(f32[2,2,128,1024]{3,1,0,2:T(2,128)} %copy.35), calls=%async_computation.3 | async-start | bytes 4194304 | tf_op jit(solution)/shard_map/all_to_all | solution.py:70
  193.6 24.8 %all-to-all-start = ((bf16[64,2,1024]{2,1,0:T(2,128)(2,1)}), bf16[64,2,1024]{2,1,0:T(2,128)(2,1)}, u32[]{:S(2)}, u32[]{:S(2)}) async-start(bf16[64,2,1024]{2,1,0:T(2,128)(2,1)} %reshape.83), calls=%async_computation | async-start | bytes 524288 | tf_op jit(solution)/shard_map/all_to_all | solution.py:57
  204.0 124.1 %reduce-scatter.2.cloned.1.call-start = ((), (), s32[]{:S(2)}) async-start(), calls=%async_computation.7 | async-start | bytes 2359296 | tf_op jit(solution)/shard_map/reduce_scatter | solution.py:87
  208.8 9.6 %copy-start.2 = (f32[1024]{0:T(1024)S(1)}, f32[1024]{0:T(1024)}, u32[]{:S(2)}) copy-start(f32[1024]{0:T(1024)} %param.7) | copy-start | bytes 12292
Sparse Core Ops, SparseCore 0:
  11.9 268.6 all-gather.1
  288.4 39.7 reduce-scatter.1
where the time goes:
time: 365 us; the launch traced here: 363 us
  waiting for transfers between devices  226 us (62%)
  starting transfers between devices  46 us (13%)
  local copies, waits for them, and re-layouts  27.6 us (8%)
  blocking collectives  26.6 us (7%)
  matrix products  22.5 us (6%)
  between operations  13.7 us (4%)
    all_gather x1, waiting for transfers between devices, body(): lax.all_gather(out_weight, 'seq', axis=0, tiled=True)  59.7 us
    all_to_all x1, waiting for transfers between devices, body(): lax.all_to_all(jnp.stack([back_re, back_im]), 'seq', split_axis=2, concat...  54.3 us
    all_to_all x1, waiting for transfers between devices, body(): lax.all_to_all(jnp.stack([turned_re, turned_im]), 'seq', split_axis=1, co...  48 us
    reduce_scatter x1, waiting for transfers between devices, body(): lax.psum_scatter(partial_out, 'chan', scatter_dimension=1, tiled=True)  39.9 us
    all_to_all x1, blocking collectives, body(): lax.all_to_all(shaped, 'seq', split_axis=0, concat_axis=1, tiled=True)  26.6 us
    all_to_all x1, starting transfers between devices, body(): lax.all_to_all(values.reshape(parts, reach, chans), 'seq', split_axis=0,...  19.2 us
    all_to_all x1, waiting for transfers between devices, body(): lax.all_to_all(values.reshape(parts, reach, chans), 'seq', split_axis=0,...  15.1 us
    all_to_all x1, starting transfers between devices, body(): lax.all_to_all(gate.reshape(parts, reach, chans), 'seq', split_axis=0, co...  10.3 us
  transfers between devices with their start and end apart: 6, of which 6 were waited for; matrix products, arithmetic and copies ran while one was open for 12% of the time, Pallas kernels for 0%

commit v1 on v0

--- a/solution.py
+++ b/solution.py
@@ -1,11 +1,78 @@
+import functools
 import math
 
 import jax
 import jax.numpy as jnp
 from jax import lax
+from jax.experimental import pallas as pl
+from jax.experimental.pallas import tpu as pltpu
 from jax.sharding import PartitionSpec as P
 
 high = lax.Precision.HIGHEST
+MESH = pl.DeviceIdType.MESH
+
+
+def wrap(a, n):
+    return jnp.where(a >= n, a - n, a)
+
+
+def each_partner(me, fn):
+    x, z, y = me // 16, (me // 8) % 2, me % 8
+    for dx in range(4):
+        for dz in range(2):
+            base = wrap(x + dx, 4) * 16 + (z if dz == 0 else 1 - z) * 8
+
+            def step(dy, carry, base=base):
+                fn(base + wrap(y + dy, 8))
+                return carry
+
+            lax.fori_loop(0 if dx or dz else 1, 8, step, 0)
+
+
+def swap_kernel(n, x_ref, o_ref, send_sem, recv_sem, own_sem):
+    me = lax.axis_index("seq")
+    bar = pltpu.get_barrier_semaphore()
+    each_partner(
+        me,
+        lambda t: pl.semaphore_signal(
+            bar, inc=1, device_id={"seq": t}, device_id_type=MESH
+        ),
+    )
+    own = pltpu.make_async_copy(x_ref.at[me], o_ref.at[me], own_sem)
+    own.start()
+    pl.semaphore_wait(bar, n - 1)
+
+    def copy(src, dst, t):
+        return pltpu.make_async_remote_copy(
+            src_ref=src,
+            dst_ref=dst,
+            send_sem=send_sem,
+            recv_sem=recv_sem,
+            device_id={"seq": t},
+            device_id_type=MESH,
+        )
+
+    each_partner(me, lambda t: copy(x_ref.at[t], o_ref.at[me], t).start())
+    own.wait()
+    rest = copy(x_ref.at[pl.ds(0, n - 1)], o_ref.at[pl.ds(0, n - 1)], me)
+    rest.wait_send()
+    rest.wait_recv()
+
+
+def swap(x, cid):
+    n = x.shape[0]
+    flat = x.reshape(n, -1, 128)
+    out = pl.pallas_call(
+        functools.partial(swap_kernel, n),
+        out_shape=jax.ShapeDtypeStruct(flat.shape, flat.dtype),
+        in_specs=[pl.BlockSpec(memory_space=pltpu.VMEM)],
+        out_specs=pl.BlockSpec(memory_space=pltpu.VMEM),
+        scratch_shapes=[pltpu.SemaphoreType.DMA] * 3,
+        compiler_params=pltpu.CompilerParams(
+            collective_id=cid, has_side_effects=True, vmem_limit_bytes=32 * 2**20
+        ),
+    )(flat)
+    return out.reshape(x.shape)
 
 
 def angle_table(rows, cols, period):
@@ -50,28 +117,22 @@
     twist = twist.astype(jnp.float32) * (2.0 * math.pi / total)
     cos_tw = jnp.cos(twist)[:, :, None]
     sin_tw = jnp.sin(twist)[:, :, None]
-    moved, gate_moved = (
-        lax.all_to_all(
-            values.reshape(parts, reach, chans), "seq", split_axis=0, concat_axis=0, tiled=True
-        ),
-        lax.all_to_all(
-            gate.reshape(parts, reach, chans), "seq", split_axis=0, concat_axis=0, tiled=True
-        ),
-    )
+    moved = swap(values.reshape(parts, reach, chans), 0)
+    gate_moved = swap(gate.reshape(parts, reach, chans), 1)
     stream = moved.astype(jnp.float32)
     part_re = jnp.einsum("ga,arc->grc", cos_ga, stream, precision=high)
     part_im = -jnp.einsum("ga,arc->grc", sin_ga, stream, precision=high)
     turned_re = part_re * cos_tw + part_im * sin_tw
     turned_im = part_im * cos_tw - part_re * sin_tw
-    freq = lax.all_to_all(
-        jnp.stack([turned_re, turned_im]), "seq", split_axis=1, concat_axis=2, tiled=True
-    )
+    turned = jnp.stack([turned_re, turned_im], axis=1).astype(jnp.bfloat16)
+    freq = swap(turned.reshape(parts, 2, 2, reach, chans), 2)
+    freq = freq.transpose(2, 1, 0, 3, 4).reshape(2, 2, tok, chans).astype(jnp.float32)
     back_re, back_im = spectral_core(freq[0], freq[1], spectrum[0], spectrum[1], cos_hr, sin_hr)
-    spread = lax.all_to_all(
-        jnp.stack([back_re, back_im]), "seq", split_axis=2, concat_axis=1, tiled=True
-    )
-    untwist_re = spread[0] * cos_tw - spread[1] * sin_tw
-    untwist_im = spread[1] * cos_tw + spread[0] * sin_tw
+    back = jnp.stack([back_re, back_im]).astype(jnp.bfloat16)
+    back = back.reshape(2, 2, parts, reach, chans).transpose(2, 1, 0, 3, 4)
+    spread = swap(back, 3).reshape(groups, 2, reach, chans).astype(jnp.float32)
+    untwist_re = spread[:, 0] * cos_tw - spread[:, 1] * sin_tw
+    untwist_im = spread[:, 1] * cos_tw + spread[:, 0] * sin_tw
     conv_part = (
         jnp.einsum("ga,grc->arc", cos_ga, untwist_re, precision=high)
         - jnp.einsum("ga,grc->arc", sin_ga, untwist_im, precision=high)
@@ -84,12 +145,10 @@
         (((1,), (1,)), ((), ())),
         preferred_element_type=jnp.float32,
     )
-    summed = lax.psum_scatter(partial_out, "chan", scatter_dimension=1, tiled=True).astype(
-        jnp.bfloat16
-    )
+    summed = lax.psum_scatter(partial_out, "chan", scatter_dimension=1, tiled=True)
     shaped = summed.reshape(parts, tok // parts, summed.shape[1])
-    returned = lax.all_to_all(shaped, "seq", split_axis=0, concat_axis=1, tiled=True)
-    return returned.reshape(tok, summed.shape[1])
+    returned = swap(shaped, 4)
+    return returned.reshape(tok, summed.shape[1]).astype(jnp.bfloat16)
 
 
 def solution(mesh):

time: 365 us -> 313 us (0.86)
  Pallas kernels: 0 us -> 148 us
  waiting for transfers between devices: 226 us -> 112 us
  starting transfers between devices: 46 us -> 0.04 us
  blocking collectives: 26.6 us -> 0 us
  local copies, waits for them, and re-layouts: 27.6 us -> 16.7 us
    pallas_call x0 -> x5, Pallas kernels: none -> 148 us  [swap(): pl.pallas_call(functools.partial(swap_kernel, n), out_shape=jax.ShapeDtyp...]
    all_to_all x4 -> x0, waiting for transfers between devices: 125 us -> none  [the longest x1 54.3 us: body(): lax.all_to_all(jnp.stack([back_re, back_im]), 'seq', split_axis=2, concat...]
    all_to_all x4 -> x0, starting transfers between devices: 45.9 us -> none  [the longest x1 19.2 us: body(): lax.all_to_all(values.reshape(parts, reach, chans), 'seq', split_axis=0,...]
    all_to_all x1 -> x0, blocking collectives: 26.6 us -> none  [body(): lax.all_to_all(shaped, 'seq', split_axis=0, concat_axis=1, tiled=True)]
    all_gather x1, waiting for transfers between devices: 59.7 us -> 71.4 us  [body(): lax.all_gather(out_weight, 'seq', axis=0, tiled=True)]
  transfers between devices with their start and end apart: 6 -> 2, of which waited for: 6 -> 2; matrix products, arithmetic and copies ran while one was open for 12% -> 10% of each run, Pallas kernels for 0% -> 41%
where the time goes in v1:
time: 313 us
  Pallas kernels  148 us (47%)
  waiting for transfers between devices  112 us (36%)
  matrix products  21 us (7%)
  local copies, waits for them, and re-layouts  16.7 us (5%)
  between operations  13.7 us (4%)
    pallas_call x5, Pallas kernels, swap(): pl.pallas_call(functools.partial(swap_kernel, n), out_shape=jax.ShapeDtyp...  148 us
    all_gather x1, waiting for transfers between devices, body(): lax.all_gather(out_weight, 'seq', axis=0, tiled=True)  71.4 us
    reduce_scatter x1, waiting for transfers between devices, body(): lax.psum_scatter(partial_out, 'chan', scatter_dimension=1, tiled=True)  39.5 us
    dot_general x1, matrix products, body(): lax.dot_general(mixed, lax.all_gather(out_weight, 'seq', axis=0, tiled=Tr...  7.61 us
  transfers between devices with their start and end apart: 2, of which 2 were waited for; matrix products, arithmetic and copies ran while one was open for 10% of the time, Pallas kernels for 41%

profile of v1, /device:TPU:6, one launch (start us, length us, event | category | flops | bytes accessed | tf_op | source)
XLA Modules:
  0.0 312.6 jit_solution(7348765398255799836)
XLA Ops:
  6.5 0.7 all-gather.2.cloned.1.call-update
  7.3 0.0 reduce-scatter.2.cloned.1.call-start
  7.3 1.1 reshape_reshape.13.x_ref
  8.4 24.7 %shard_map.56 = bf16[64,16,128]{2,1,0:T(8,128)(2,1)S(1)} custom-call(bf16[64,16,128]{2,1,0:T(8,128)(2,1)S(1)} %reshape_reshape.13.x_ref), custom_call_target="tpu_custom_call" | custom-call | tf_op jit(solution)/shard_map/pallas_call | solution.py:65
  33.1 0.1 reshape.88
  33.2 0.1 fusion.76
  33.3 0.8 convolution_negate_fusion
  34.1 0.9 fusion.19
  35.0 0.1 pad_maximum_fusion
  35.1 1.1 copy.25
  36.2 0.7 convert_element_type.72.x_ref
  36.9 38.8 %shard_map.57 = bf16[64,64,128]{2,1,0:T(8,128)(2,1)S(1)} custom-call(bf16[64,64,128]{2,1,0:T(8,128)(2,1)S(1)} %convert_element_type.72.x_ref), custom_call_target="tpu_custom_call" | custom-call | tf_op jit(solution)/shard_map/pallas_call | solution.py:65
  75.7 0.3 reshape.89
  76.0 0.8 copy.77
  76.9 0.7 fusion.127
  77.6 0.5 copy.27
  78.2 0.7 copy.28
  78.9 1.7 fusion.126
  80.6 1.3 copy.49
  81.9 1.4 copy.50
  83.3 0.8 fusion.41
  84.1 0.8 fusion.39
  85.0 0.8 fusion.1
  85.8 1.0 fusion.10
  86.8 1.3 fusion.37
  88.1 1.3 fusion.5
  89.4 0.2 stack.24
  89.6 1.3 fusion.35
  90.9 1.3 fusion.4
  92.2 0.2 stack.25
  92.4 1.3 copy_bitcast_fusion.2
  93.7 0.7 reshape.90.x_ref
  94.4 40.2 %shard_map.58 = bf16[64,64,128]{2,1,0:T(8,128)(2,1)S(1)} custom-call(bf16[64,64,128]{2,1,0:T(8,128)(2,1)S(1)} %reshape.90.x_ref), custom_call_target="tpu_custom_call" | custom-call | tf_op jit(solution)/shard_map/pallas_call | solution.py:65
  134.7 1.1 reshape.93
  135.7 1.1 reshape_reshape.12.x_ref
  136.8 25.0 %shard_map.55 = bf16[64,16,128]{2,1,0:T(8,128)(2,1)S(1)} custom-call(bf16[64,16,128]{2,1,0:T(8,128)(2,1)S(1)} %reshape_reshape.12.x_ref), custom_call_target="tpu_custom_call" | custom-call | tf_op jit(solution)/shard_map/pallas_call | solution.py:65
  161.8 0.3 reshape.92
  162.1 0.8 fusion.125
  162.9 1.4 fusion.15
  164.3 1.6 fusion.9
  166.0 0.3 copy.43
  166.2 0.1 reshape.91
  166.3 71.4 %all-gather.2.cloned.1.call-done = bf16[4096,1024]{1,0:T(8,128)(2,1)} async-done(((bf16[64,1024]{1,0:T(8,128)(2,1)}), bf16[4096,1024]{1,0:T(8,128)(2,1)}) %all-gather.2.cloned.1.call-update) | async-done | bytes 8388624 | tf_op jit(solution)/shard_map/all_gather | solution.py:144
  237.7 7.6 %fusion.132 = f32[128,4096]{1,0:T(8,128)} fusion(bf16[128,1024]{1,0:T(8,128)(2,1)S(1)} %reshape.91, bf16[4096,1024]{1,0:T(8,128)(2,1)} %all-gather.2.cloned.1.call-done), kind=kOutput, calls=%fused_computation.144 | convolution fusion | flops 1073741824 | bytes 10747904 | tf_op jit(solution)/shard_map/dot_general | solution.py:142
  245.3 39.5 %reduce-scatter.2.cloned.1.call-done = f32[128,512]{1,0:T(8,128)} async-done(((f32[128,4096]{1,0:T(8,128)}), f32[128,512]{1,0:T(8,128)}) %reduce-scatter.2.cloned.1.call-update) | async-done | bytes 262160 | tf_op jit(solution)/shard_map/reduce_scatter | solution.py:148
  284.9 1.0 reshape_reshape.14.x_ref
  285.8 19.1 %shard_map.59 = f32[64,8,128]{2,1,0:T(8,128)S(1)} custom-call(f32[64,8,128]{2,1,0:T(8,128)S(1)} %reshape_reshape.14.x_ref), custom_call_target="tpu_custom_call" | custom-call | tf_op jit(solution)/shard_map/pallas_call | solution.py:65
  305.0 0.7 convert_element_type.79
  (10 shorter events, 0.1 us)
Async XLA Ops:
  6.5 231.2 %all-gather.2.cloned.1.call-start = ((), (), s32[]{:S(2)}) async-start(), calls=%async_computation.1 | async-start | bytes 8519680 | tf_op jit(solution)/shard_map/all_gather | solution.py:144
  7.3 277.6 %reduce-scatter.2.cloned.1.call-start = ((), (), s32[]{:S(2)}) async-start(), calls=%async_computation.2 | async-start | bytes 2359296 | tf_op jit(solution)/shard_map/reduce_scatter | solution.py:148
  84.1 1.7 copy-start
  84.1 1.7 copy-start.1
  162.9 1.4 copy-start.2
Sparse Core Ops, SparseCore 0:
  11.9 225.8 all-gather.1
  245.5 39.3 reduce-scatter.1

commit v2 on v0

v2 whole, which is shorter than its diff:
```python
import functools
import math

import jax
import jax.numpy as jnp
import numpy as np
from jax import lax
from jax.experimental import pallas as pl
from jax.experimental.pallas import tpu as pltpu
from jax.sharding import PartitionSpec as P

MESH = pl.DeviceIdType.MESH
BF = jnp.bfloat16
F32 = jnp.float32
SEQ = 64
GRP = 72


def wrap(a, n):
    return jnp.where(a >= n, a - n, a)


def split(x):
    top = x.astype(BF)
    return top, (x - top.astype(F32)).astype(BF)


def tables():
    g = np.arange(GRP)
    live = (g <= 64).astype(np.float64)[:, None]
    a = np.arange(SEQ)
    turn = 2.0 * np.pi * ((g[:, None] * a[None, :]) % 128) / 128
    ahead = np.concatenate([np.cos(turn) * live, -np.sin(turn) * live])
    top = ahead.astype(BF)
    low = (ahead - top.astype(np.float64)).astype(BF)
    ahead = np.concatenate([top, low], axis=1)
    back = np.concatenate([np.cos(turn) * live, -np.sin(turn) * live]).T / 16384.0
    top = back.astype(BF)
    low = (back - top.astype(np.float64)).astype(BF)
    back = np.concatenate([top, top, low], axis=1)
    lane = np.arange(128)
    i_of = lane // 16
    r = 16 * i_of[None, None, :] + np.arange(16)[:, None, None]
    theta = 2.0 * np.pi * ((r * g[None, :, None]) % 16384) / 16384
    twist = np.stack([np.cos(theta), -np.sin(theta)], axis=1).astype(np.float32)
    same = (lane[:, None] % 16 == lane[None, :] % 16).astype(np.float64)
    turn = 2.0 * np.pi * ((i_of[:, None] * i_of[None, :]) % 8) / 8
    c, s = np.cos(turn) * same, np.sin(turn) * same
    lane_ahead = np.block([[c, -s], [s, c]])
    lane_back = np.block([[c, s], [-s, c]])
    lane_ahead = np.concatenate([lane_ahead, lane_ahead]).astype(BF)
    lane_back = np.concatenate([lane_back, lane_back]).astype(BF)
    turn = 2.0 * np.pi * (np.arange(16)[:, None] * i_of[None, :]) / 128
    small = np.stack([np.cos(turn), -np.sin(turn)]).astype(np.float32)
    return ahead, back, twist, lane_ahead, lane_back, small


def swap_lanes(x):
    x = list(x)
    block = lax.broadcasted_iota(jnp.int32, x[0].shape, 1) // 16
    for bit in (1, 2, 4):
        clear = (block // bit) % 2 == 0
        for p in range(8):
            if p & bit:
                continue
            q = p | bit
            u, v = x[p], x[q]
            x[p] = jnp.where(clear, u, pltpu.roll(v, 16 * bit, 1))
            x[q] = jnp.where(clear, pltpu.roll(u, 128 - 16 * bit, 1), v)
    return x


def fft(z, sign):
    n = len(z)
    if n == 1:
        return z
    even, odd = fft(z[0::2], sign), fft(z[1::2], sign)
    out = [None] * n
    for k in range(n // 2):
        re, im = odd[k]
        if k == 0:
            pass
        elif 4 * k == n:
            re, im = (-im, re) if sign > 0 else (im, -re)
        elif 8 * k == n or 8 * k == 3 * n:
            h = math.sqrt(0.5)
            c = h if 8 * k == n else -h
            if sign > 0:
                re, im = re * c - im * h, im * c + re * h
            else:
                re, im = re * c + im * h, im * c - re * h
        else:
            c = math.cos(2 * math.pi * k / n)
            s = sign * math.sin(2 * math.pi * k / n)
            re, im = re * c - im * s, re * s + im * c
        out[k] = (even[k][0] + re, even[k][1] + im)
        out[k + n // 2] = (even[k][0] - re, even[k][1] - im)
    return out


def conv_kernel(
    values_hbm, gate_hbm, skip_hbm, spec_hbm,
    ahead_hbm, back_hbm, twist_hbm, lane_ahead_hbm, lane_back_hbm, small_hbm,
    out_ref,
    values_ref, gate_ref, skip_ref, spec_ref,
    ahead_ref, back_ref, twist_ref, lane_ahead_ref, lane_back_ref, small_ref,
    send_v, recv_v, send_k, recv_k, send_c, recv_c,
    time_ref, low_ref, high_ref, first_ref, second_ref,
    in_sem, spec_sem, own_sem, send_sem, recv_sem,
):
    me = lax.axis_index("seq")
    x, z, y = me // 16, (me // 8) % 2, me % 8

    def other(dx, dz, dy):
        zt = z + dz - 2 * z * dz
        return wrap(x + dx, 4) * 16 + zt * 8 + wrap(y + dy, 8)

    def each_partner(fn):
        def step(i, carry):
            dx, dz, dy = i // 16, (i // 8) % 2, i % 8
            fn(other(dx, dz, dy))
            return carry

        lax.fori_loop(1, SEQ, step, 0)

    loads = []
    for at, (src, dst) in enumerate((
        (values_hbm, values_ref), (gate_hbm, gate_ref), (skip_hbm, skip_ref),
        (ahead_hbm, ahead_ref), (back_hbm, back_ref), (twist_hbm, twist_ref),
        (lane_ahead_hbm, lane_ahead_ref), (lane_back_hbm, lane_back_ref),
        (small_hbm, small_ref),
    )):
        load = pltpu.make_async_copy(src, dst, in_sem.at[at])
        load.start()
        loads.append(load)
    spec_loads = []
    for lt in range(8):
        load = pltpu.make_async_copy(
            spec_hbm.at[:, :, :, pl.ds(128 * lt, 128)], spec_ref.at[lt], spec_sem.at[lt]
        )
        load.start()
        spec_loads.append(load)

    bar = pltpu.get_barrier_semaphore()
    each_partner(
        lambda t: pl.semaphore_signal(
            bar, inc=1, device_id={"seq": t}, device_id_type=MESH
        )
    )

    def lanes(lt):
        return pl.ds(pl.multiple_of(128 * lt, 128), 128)

    def remote(src, dst, t, at):
        return pltpu.make_async_remote_copy(
            src_ref=src, dst_ref=dst, send_sem=send_sem.at[at], recv_sem=recv_sem.at[at],
            device_id={"seq": t}, device_id_type=MESH,
        )

    def all_sent(src, at):
        remote(src.at[pl.ds(0, SEQ - 1)], src.at[pl.ds(0, SEQ - 1)], me, at).wait_send()

    def all_here(dst, at):
        remote(dst.at[pl.ds(0, SEQ - 1)], dst.at[pl.ds(0, SEQ - 1)], me, at).wait_recv()

    loads[0].wait()

    def pack_values(lt, carry):
        tiles = swap_lanes(
            [values_ref[16 * i : 16 * i + 16, lanes(lt)].astype(F32) for i in range(8)]
        )
        for d in range(8):
            send_v[lt * 8 + d] = tiles[d].astype(BF)
        return carry

    lax.fori_loop(0, 8, pack_values, 0)
    own_v = pltpu.make_async_copy(send_v.at[me], recv_v.at[me], own_sem.at[0])
    own_v.start()
    pl.semaphore_wait(bar, SEQ - 1)
    each_partner(lambda t: remote(send_v.at[t], recv_v.at[me], t, 0).start())

    upper = me >= SEQ // 2
    slot = jnp.where(upper, 95 - me, me)
    for load in spec_loads:
        load.wait()

    def pack_spectrum(i, carry):
        dx, dz = i // 2, i % 2
        lt = wrap(x + dx, 4) * 2 + z + dz - 2 * z * dz

        def plane(q, inner):
            gl, part = q // 2, q % 2
            source = jnp.where(upper, 1 - gl, gl)
            tiles = swap_lanes([
                spec_ref[lt, part, source, pl.ds(jnp.where(upper, 7 - h, h), 16, stride=8), :]
                for h in range(8)
            ])
            for d in range(8):
                send_k[lt * 8 + d, pl.ds(pl.multiple_of(16 * q, 16), 16), :] = tiles[d].astype(BF)
            return inner

        lax.fori_loop(0, 4, plane, 0)

        @pl.when(i > 0)
        def _():
            t = lt * 8 + y
            remote(send_k.at[t], recv_k.at[slot], t, 1).start()

        def to_row(dy, inner):
            t = lt * 8 + wrap(y + dy, 8)
            remote(send_k.at[t], recv_k.at[slot], t, 1).start()
            return inner

        lax.fori_loop(1, 8, to_row, 0)
        return carry

    lax.fori_loop(0, 8, pack_spectrum, 0)
    own_k = pltpu.make_async_copy(send_k.at[me], recv_k.at[slot], own_sem.at[1])
    own_k.start()
    for load in loads[1:]:
        load.wait()

    own_v.wait()
    all_here(recv_v, 0)
    time_ref[...] = recv_v[...].reshape(SEQ * 16, 128).astype(F32)

    def over_a(jj, carry):
        pair = jnp.concatenate(
            [time_ref[pl.ds(2 * jj + b, SEQ, stride=16), :].astype(BF) for b in range(2)], axis=1
        )
        both = jnp.concatenate([pair, pair], axis=0)
        got = jnp.dot(ahead_ref[...], both, preferred_element_type=F32)
        for b in range(2):
            re, im = got[:GRP, 128 * b : 128 * b + 128], got[GRP:, 128 * b : 128 * b + 128]
            tr, ti = twist_ref[2 * jj + b, 0], twist_ref[2 * jj + b, 1]
            rows = pl.ds(pl.multiple_of((2 * jj + b) * GRP, 8), GRP)
            first_ref[rows, 0:128] = re * tr - im * ti
            first_ref[rows, 128:256] = re * ti + im * tr
        return carry

    lax.fori_loop(0, 8, over_a, 0)

    def over_lanes(src, table, dst):
        def step(b, carry):
            rows = pl.ds(pl.multiple_of(b * 288, 16), 288)
            top, low = split(src[rows, :])
            dst[rows, :] = jnp.dot(
                jnp.concatenate([top, low], axis=1), table[...], preferred_element_type=F32
            )
            return carry

        lax.fori_loop(0, 4, step, 0)

    over_lanes(first_ref, lane_ahead_ref, second_ref)

    own_k.wait()
    all_here(recv_k, 1)
    low_ref[pl.ds(64 * 32, 8 * 32), :] = jnp.zeros((8 * 32, 128), F32)
    high_ref[pl.ds(0, 32), :] = jnp.zeros((32, 128), F32)
    high_ref[pl.ds(65 * 32, 7 * 32), :] = jnp.zeros((7 * 32, 128), F32)

    def widen(b, carry):
        rows = pl.multiple_of(b * 256, 32)
        low_ref[pl.ds(rows, 256), :] = recv_k[pl.ds(4 * b, 4)].reshape(256, 128).astype(F32)
        high_ref[pl.ds(32 + rows, 256), :] = (
            recv_k[pl.ds(32 + 4 * b, 4)].reshape(256, 128).astype(F32)
        )
        return carry

    lax.fori_loop(0, 8, widen, 0)

    def filtered(b, carry):
        g = b * 8

        def rows(j):
            return pl.ds(pl.multiple_of(j * GRP + g, 8), 8)

        turned = []
        for j in range(16):
            re, im = second_ref[rows(j), 0:128], second_ref[rows(j), 128:256]
            if j:
                tr, ti = small_ref[0, j : j + 1, :], small_ref[1, j : j + 1, :]
                re, im = re * tr - im * ti, re * ti + im * tr
            turned.append((re, im))
        freq = fft(turned, -1)
        prod = []
        for h in range(16):
            re, im = freq[h]
            kr = (
                low_ref[pl.ds(g * 32 + h, 8, stride=32), :]
                + high_ref[pl.ds(g * 32 + 15 - h, 8, stride=32), :]
            )
            ki = (
                low_ref[pl.ds(g * 32 + 16 + h, 8, stride=32), :]
                - high_ref[pl.ds(g * 32 + 31 - h, 8, stride=32), :]
            )
            prod.append((re * kr - im * ki, re * ki + im * kr))
        spread = fft(prod, 1)
        for j in range(16):
            re, im = spread[j]
            if j:
                tr, ti = small_ref[0, j : j + 1, :], small_ref[1, j : j + 1, :]
                re, im = re * tr + im * ti, im * tr - re * ti
            first_ref[rows(j), 0:128] = re
            first_ref[rows(j), 128:256] = im
        return carry

    lax.fori_loop(0, GRP // 8, filtered, 0)
    over_lanes(first_ref, lane_back_ref, second_ref)

    def back_over_a(jj, carry):
        sides = []
        for b in range(2):
            rows = pl.ds(pl.multiple_of((2 * jj + b) * GRP, 8), GRP)
            re, im = second_ref[rows, 0:128], second_ref[rows, 128:256]
            tr, ti = twist_ref[2 * jj + b, 0], twist_ref[2 * jj + b, 1]
            sides.append(jnp.concatenate([re * tr + im * ti, im * tr - re * ti], axis=0))
        top, low = split(jnp.concatenate(sides, axis=1))
        got = jnp.dot(
            back_ref[...], jnp.concatenate([top, low, top], axis=0), preferred_element_type=F32
        )
        for b in range(2):
            time_ref[pl.ds(2 * jj + b, SEQ, stride=16), :] = got[:, 128 * b : 128 * b + 128]
        return carry

    lax.fori_loop(0, 8, back_over_a, 0)
    send_c[...] = time_ref[...].astype(BF).reshape(SEQ, 16, 128)
    own_c = pltpu.make_async_copy(send_c.at[me], recv_c.at[me], own_sem.at[2])
    own_c.start()
    each_partner(lambda t: remote(send_c.at[t], recv_c.at[me], t, 2).start())
    own_c.wait()
    all_here(recv_c, 2)

    def mix(lt, carry):
        tiles = swap_lanes([recv_c[lt * 8 + d].astype(F32) for d in range(8)])
        scale = skip_ref[0:1, lanes(lt)]
        for i in range(8):
            rows = slice(16 * i, 16 * i + 16)
            held = values_ref[rows, lanes(lt)].astype(F32)
            out_ref[rows, lanes(lt)] = (
                gate_ref[rows, lanes(lt)].astype(F32) * (tiles[i] + scale * held)
            ).astype(BF)
        return carry

    lax.fori_loop(0, 8, mix, 0)
    all_sent(send_v, 0)
    all_sent(send_k, 1)
    all_sent(send_c, 2)


def long_conv(values, gate, skip, spectrum):
    consts = [jnp.asarray(t) for t in tables()]
    arrays = [values, gate, skip.reshape(1, -1), spectrum] + consts
    vmem = lambda t: pltpu.VMEM(t.shape, t.dtype)
    held = [vmem(a) for a in arrays[:3]] + [pltpu.VMEM((8, 2, 2, 128, 128), F32)]
    held += [vmem(t) for t in consts]
    dma = pltpu.SemaphoreType.DMA
    return pl.pallas_call(
        conv_kernel,
        out_shape=jax.ShapeDtypeStruct(values.shape, BF),
        in_specs=[pl.BlockSpec(memory_space=pl.ANY)] * len(arrays),
        out_specs=pl.BlockSpec(memory_space=pltpu.VMEM),
        scratch_shapes=held
        + [pltpu.VMEM((SEQ, 16, 128), BF)] * 2
        + [pltpu.VMEM((SEQ, 64, 128), BF)] * 2
        + [pltpu.VMEM((SEQ, 16, 128), BF)] * 2
        + [pltpu.VMEM((SEQ * 16, 128), F32)]
        + [pltpu.VMEM((GRP * 32, 128), F32)] * 2
        + [pltpu.VMEM((GRP * 16, 256), F32)] * 2
        + [dma((9,)), dma((8,)), dma((3,)), dma((3,)), dma((3,))],
        compiler_params=pltpu.CompilerParams(
            collective_id=0, has_side_effects=True, vmem_limit_bytes=40 * 2**20
        ),
        name="long_conv",
    )(*arrays)


def body(values, gate, skip, spectrum, out_weight):
    mixed = long_conv(values, gate, skip, spectrum)
    partial_out = lax.dot_general(
        mixed,
        lax.all_gather(out_weight, "seq", axis=0, tiled=True),
        (((1,), (1,)), ((), ())),
        preferred_element_type=F32,
    )
    return lax.psum_scatter(partial_out, "chan", scatter_dimension=1, tiled=True).astype(BF)


def solution(mesh):
    placed = (
        P("seq", "chan"),
        P("seq", "chan"),
        P("chan"),
        P(None, "seq", None, "chan"),
        P("seq", "chan"),
    )
    return jax.shard_map(
        body, mesh=mesh, in_specs=placed, out_specs=P("seq", "chan"), check_vma=False
    )
```

time: 365 us -> 287 us (0.79)
  Pallas kernels: 0 us -> 70.9 us
  starting transfers between devices: 46 us -> 0.04 us
  waiting for transfers between devices: 226 us -> 184 us
  blocking collectives: 26.6 us -> 0 us
  local copies, waits for them, and re-layouts: 27.6 us -> 9.66 us
  matrix products: 22.5 us -> 7.6 us
    all_to_all x4 -> x0, waiting for transfers between devices: 125 us -> none  [the longest x1 54.3 us: body(): lax.all_to_all(jnp.stack([back_re, back_im]), 'seq', split_axis=2, concat...]
    all_gather x1, waiting for transfers between devices: 59.7 us -> 145 us  [body(): lax.all_gather(out_weight, 'seq', axis=0, tiled=True)]
    pallas_call x0 -> x1, Pallas kernels: none -> 70.9 us  [long_conv(): pl.pallas_call(conv_kernel, out_shape=jax.ShapeDtypeStruct(values.shape,...]
    all_to_all x4 -> x0, starting transfers between devices: 45.9 us -> none  [the longest x1 19.2 us: body(): lax.all_to_all(values.reshape(parts, reach, chans), 'seq', split_axis=0,...]
    all_to_all x1 -> x0, blocking collectives: 26.6 us -> none  [body(): lax.all_to_all(shaped, 'seq', split_axis=0, concat_axis=1, tiled=True)]
    dot_general x12 -> x0, matrix products: 14.8 us -> none  [the longest x1 2.07 us: body(): jnp.einsum('ga,grc->arc', sin_ga, untwist_im, precision=high)]
    slice x5 -> x0, local copies, waits for them, and re-layouts: 8.32 us -> none  [the longest x3 3.27 us: body(): untwist_re = spread[0] * cos_tw - spread[1] * sin_tw]
    unnamed x8 -> x20, local copies, waits for them, and re-layouts: 4.11 us -> 9.66 us
  transfers between devices with their start and end apart: 6 -> 2, of which waited for: 6 -> 2; matrix products, arithmetic and copies ran while one was open for 12% -> 0% of each run, Pallas kernels for 0% -> 25%
where the time goes in v2:
time: 287 us
  waiting for transfers between devices  184 us (64%)
  Pallas kernels  70.9 us (25%)
  between operations  13.4 us (5%)
  local copies, waits for them, and re-layouts  9.66 us (3%)
  matrix products  7.6 us (3%)
    all_gather x1, waiting for transfers between devices, body(): lax.all_gather(out_weight, 'seq', axis=0, tiled=True)  145 us
    pallas_call x1, Pallas kernels, long_conv(): pl.pallas_call(conv_kernel, out_shape=jax.ShapeDtypeStruct(values.shape,...  70.9 us
    reduce_scatter x1, waiting for transfers between devices, body(): lax.psum_scatter(partial_out, 'chan', scatter_dimension=1, tiled=True)  38.4 us
    unnamed x20, local copies, waits for them, and re-layouts  9.66 us
    dot_general x1, matrix products, body(): lax.dot_general(mixed, lax.all_gather(out_weight, 'seq', axis=0, tiled=Tr...  7.6 us
  transfers between devices with their start and end apart: 2, of which 2 were waited for; matrix products, arithmetic and copies ran while one was open for 0% of the time, Pallas kernels for 25%

profile of v2, /device:TPU:6, one launch (start us, length us, event | category | flops | bytes accessed | tf_op | source)
XLA Modules:
  0.0 286.9 jit_solution(13547440792880463694)
XLA Ops:
  6.5 0.0 all-gather.2.cloned.1.call-start
  6.5 0.7 all-gather.2.cloned.1.call-update
  7.3 0.0 reduce-scatter.2.cloned.1.call-start
  7.3 0.0 copy-start
  7.3 1.6 copy-done
  8.9 0.0 copy-start.1
  8.9 1.3 copy-done.1
  10.2 0.0 copy-start.2
  10.2 0.9 copy-done.2
  11.1 0.0 copy-start.3
  11.1 0.9 copy-done.3
  12.1 0.0 copy-start.4
  12.1 0.9 copy-done.4
  13.0 0.0 copy-start.5
  13.0 0.9 copy-done.5
  14.0 0.0 copy-start.6
  14.0 0.8 copy-done.6
  14.8 0.0 copy-start.7
  14.8 0.8 copy-done.7
  15.6 0.0 copy-start.8
  15.6 0.7 copy-done.8
  16.3 0.0 copy-start.9
  16.3 0.7 copy-done.9
  17.0 70.9 %long_conv.1 = bf16[128,1024]{1,0:T(8,128)(2,1)S(1)} custom-call(bf16[128,1024]{1,0:T(8,128)(2,1)S(1)} %copy-done.2, bf16[128,1024]{1,0:T(8,128)(2,1)S(1)} %copy-done.3, f32[1,1024]{1,0:T(1,128)S(1)} %bitcast.3, f32[2,2,128,1024]{3,2,1,0:T(8,128)S(1)} %copy-done, bf16[144,128]{1,0:T(8,128)(2,1)S(1)} %copy-done.7, bf16[64,432]{1,0:T(8,128)(2,1)S(1)} %copy-done.6, ...), custom_call_target="tpu_custom_call" | custom-call | tf_op jit(solution)/shard_map/long_conv/pallas_call | solution.py:358
  87.9 144.5 %all-gather.2.cloned.1.call-done = bf16[4096,1024]{1,0:T(8,128)(2,1)} async-done(((bf16[64,1024]{1,0:T(8,128)(2,1)}), bf16[4096,1024]{1,0:T(8,128)(2,1)}) %all-gather.2.cloned.1.call-update) | async-done | bytes 8388624 | tf_op jit(solution)/shard_map/all_gather | solution.py:382
  232.4 7.6 %fusion = f32[128,4096]{1,0:T(8,128)} fusion(bf16[128,1024]{1,0:T(8,128)(2,1)S(1)} %long_conv.1, bf16[4096,1024]{1,0:T(8,128)(2,1)} %all-gather.2.cloned.1.call-done), kind=kOutput, calls=%fused_computation | convolution fusion | flops 1073741824 | bytes 10747904 | tf_op jit(solution)/shard_map/dot_general | solution.py:380
  240.0 0.0 reduce-scatter.2.cloned.1.call-update
  240.0 38.4 %reduce-scatter.2.cloned.1.call-done = f32[128,512]{1,0:T(8,128)} async-done(((f32[128,4096]{1,0:T(8,128)}), f32[128,512]{1,0:T(8,128)}) %reduce-scatter.2.cloned.1.call-update) | async-done | bytes 262160 | tf_op jit(solution)/shard_map/reduce_scatter | solution.py:386
  278.4 1.6 convert_element_type.3
Async XLA Ops:
  6.5 225.8 %all-gather.2.cloned.1.call-start = ((), (), s32[]{:S(2)}) async-start(), calls=%async_computation.1 | async-start | bytes 8519680 | tf_op jit(solution)/shard_map/all_gather | solution.py:382
  7.3 271.1 %reduce-scatter.2.cloned.1.call-start = ((), (), s32[]{:S(2)}) async-start(), calls=%async_computation.2 | async-start | bytes 2359296 | tf_op jit(solution)/shard_map/reduce_scatter | solution.py:386
  7.3 1.6 copy-start
  8.9 1.3 copy-start.1
  10.2 0.9 copy-start.2
  11.1 0.9 copy-start.3
  12.1 0.9 copy-start.4
  13.0 0.9 copy-start.5
  14.0 0.8 copy-start.6
  14.8 0.8 copy-start.7
  15.6 0.7 copy-start.8
  16.3 0.7 copy-start.9
Sparse Core Ops, SparseCore 0:
  11.9 220.4 all-gather.1
  240.1 38.2 reduce-scatter.1

commit v3 on v2

--- a/solution.py
+++ b/solution.py
@@ -98,18 +98,23 @@
     return out
 
 
-def conv_kernel(
-    values_hbm, gate_hbm, skip_hbm, spec_hbm,
+def block_kernel(
+    values_hbm, gate_hbm, skip_hbm, spec_hbm, weight_hbm,
     ahead_hbm, back_hbm, twist_hbm, lane_ahead_hbm, lane_back_hbm, small_hbm,
     out_ref,
     values_ref, gate_ref, skip_ref, spec_ref,
     ahead_ref, back_ref, twist_ref, lane_ahead_ref, lane_back_ref, small_ref,
     send_v, recv_v, send_k, recv_k, send_c, recv_c,
     time_ref, low_ref, high_ref, first_ref, second_ref,
+    w_ref, mixed_ref, recv_m, half_send, half_recv, own_half, z_send, z_recv, done,
     in_sem, spec_sem, own_sem, send_sem, recv_sem,
+    ring_send, ring_recv, m_send, m_recv, h_send, h_recv, zs_sem, zr_sem, o_sem,
 ):
-    me = lax.axis_index("seq")
+    me, ch = lax.axis_index("seq"), lax.axis_index("chan")
     x, z, y = me // 16, (me // 8) % 2, me % 8
+    low = me % 16
+    zl, core = ch // 2, ch % 2
+    cross = x != zl
 
     def other(dx, dz, dy):
         zt = z + dz - 2 * z * dz
@@ -142,11 +147,26 @@
         spec_loads.append(load)
 
     bar = pltpu.get_barrier_semaphore()
-    each_partner(
-        lambda t: pl.semaphore_signal(
-            bar, inc=1, device_id={"seq": t}, device_id_type=MESH
-        )
-    )
+
+    def greet(seq, chan):
+        pl.semaphore_signal(
+            bar, inc=1, device_id={"seq": seq, "chan": chan}, device_id_type=MESH
+        )
+
+    each_partner(lambda t: greet(t, ch))
+    for d in (1, 2, 3):
+        greet(me, wrap(zl + d, 4) * 2 + core)
+    greet(me, zl * 2 + 1 - core)
+
+    @pl.when(cross)
+    def _():
+        greet(zl * 16 + low, x * 2 + core)
+
+    def link(src, dst, ss, rs, seq, chan):
+        return pltpu.make_async_remote_copy(
+            src_ref=src, dst_ref=dst, send_sem=ss, recv_sem=rs,
+            device_id={"seq": seq, "chan": chan}, device_id_type=MESH,
+        )
 
     def lanes(lt):
         return pl.ds(pl.multiple_of(128 * lt, 128), 128)
@@ -176,7 +196,14 @@
     lax.fori_loop(0, 8, pack_values, 0)
     own_v = pltpu.make_async_copy(send_v.at[me], recv_v.at[me], own_sem.at[0])
     own_v.start()
-    pl.semaphore_wait(bar, SEQ - 1)
+    pl.semaphore_wait(bar, jnp.where(cross, SEQ + 4, SEQ + 3))
+    own_w = pltpu.make_async_copy(weight_hbm, w_ref.at[z, y], own_sem.at[3])
+    own_w.start()
+    pair_w = link(
+        weight_hbm, w_ref.at[z, y], ring_send.at[0, 0], ring_recv.at[0, 0],
+        x * 16 + (1 - z) * 8 + y, ch,
+    )
+    pair_w.start()
     each_partner(lambda t: remote(send_v.at[t], recv_v.at[me], t, 0).start())
 
     upper = me >= SEQ // 2
@@ -220,8 +247,25 @@
     for load in loads[1:]:
         load.wait()
 
+    def ring(step, way):
+        at = wrap(y + (9 - step if way == 0 else step - 1), 8)
+        block = w_ref.at[:, at] if step < 4 else w_ref.at[way, at]
+        to = wrap(y + (1 if way == 0 else 7), 8)
+        return link(
+            block, block, ring_send.at[way, step], ring_recv.at[way, step], x * 16 + z * 8 + to, ch
+        )
+
+    def ring_step(step):
+        for way in range(2):
+            if step > 1:
+                ring(step - 1, way).wait_recv()
+            ring(step, way).start()
+
     own_v.wait()
     all_here(recv_v, 0)
+    own_w.wait()
+    pair_w.wait_recv()
+    ring_step(1)
     time_ref[...] = recv_v[...].reshape(SEQ * 16, 128).astype(F32)
 
     def over_a(jj, carry):
@@ -255,6 +299,7 @@
 
     own_k.wait()
     all_here(recv_k, 1)
+    ring_step(2)
     low_ref[pl.ds(64 * 32, 8 * 32), :] = jnp.zeros((8 * 32, 128), F32)
     high_ref[pl.ds(0, 32), :] = jnp.zeros((32, 128), F32)
     high_ref[pl.ds(65 * 32, 7 * 32), :] = jnp.zeros((7 * 32, 128), F32)
@@ -328,8 +373,10 @@
     own_c = pltpu.make_async_copy(send_c.at[me], recv_c.at[me], own_sem.at[2])
     own_c.start()
     each_partner(lambda t: remote(send_c.at[t], recv_c.at[me], t, 2).start())
+    ring_step(3)
     own_c.wait()
     all_here(recv_c, 2)
+    ring_step(4)
 
     def mix(lt, carry):
         tiles = swap_lanes([recv_c[lt * 8 + d].astype(F32) for d in range(8)])
@@ -337,28 +384,108 @@
         for i in range(8):
             rows = slice(16 * i, 16 * i + 16)
             held = values_ref[rows, lanes(lt)].astype(F32)
-            out_ref[rows, lanes(lt)] = (
+            mixed_ref[rows, lanes(lt)] = (
                 gate_ref[rows, lanes(lt)].astype(F32) * (tiles[i] + scale * held)
             ).astype(BF)
         return carry
 
     lax.fori_loop(0, 8, mix, 0)
+    for d in (1, 3, 2):
+        link(
+            mixed_ref, recv_m.at[d], m_send.at[d], m_recv.at[d], wrap(x + d, 4) * 16 + low, ch
+        ).start()
+    for way in range(2):
+        ring(4, way).wait_recv()
+    order = (0, 1, 3, 2)
+
+    def half_copy(d):
+        return link(
+            half_send.at[d], half_recv.at[d], h_send.at[d], h_recv.at[d], me, zl * 2 + 1 - core
+        )
+
+    def multiply(d):
+        src = mixed_ref
+        if d:
+            link(mixed_ref, recv_m.at[d], m_send.at[d], m_recv.at[d], me, ch).wait_recv()
+            src = recv_m.at[d]
+        for side in range(2):
+            half = 1 - core if side == 0 else core
+            got = lax.dot_general(
+                src[...], w_ref[half].reshape(512, 1024), (((1,), (1,)), ((), ())),
+                preferred_element_type=F32,
+            )
+            if side == 0:
+                half_send[d] = got.astype(BF)
+                half_copy(d).start()
+            else:
+                own_half[d] = got
+
+    def pass_on(d):
+        half_copy(d).wait_recv()
+        target = wrap(x + 4 - d, 4)
+        total = own_half[d] + half_recv[d].astype(F32)
+
+        @pl.when(target == zl)
+        def _():
+            done[...] = total
+
+        @pl.when(target != zl)
+        def _():
+            z_send[d] = total.astype(BF)
+            link(
+                z_send.at[d], z_recv.at[zl], zs_sem.at[d], zr_sem.at[zl], me, target * 2 + core
+            ).start()
+
+    for at, d in enumerate(order):
+        multiply(d)
+        if at:
+            pass_on(order[at - 1])
+    pass_on(order[-1])
+    for d in (1, 2, 3):
+        peer = wrap(zl + d, 4)
+        link(z_send.at[0], z_recv.at[peer], zs_sem.at[0], zr_sem.at[peer], me, ch).wait_recv()
+        done[...] += z_recv[peer].astype(F32)
+
+    @pl.when(cross)
+    def _():
+        z_send[4] = done[...].astype(BF)
+        last = link(z_send.at[4], out_ref, o_sem.at[0], o_sem.at[1], zl * 16 + low, x * 2 + core)
+        last.start()
+        last.wait()
+
+    @pl.when(jnp.logical_not(cross))
+    def _():
+        out_ref[...] = done[...].astype(BF)
+
+    for d in range(4):
+        half_copy(d).wait_send()
+
+        @pl.when(wrap(x + 4 - d, 4) != zl)
+        def _(d=d):
+            link(z_send.at[d], z_recv.at[0], zs_sem.at[d], zr_sem.at[0], me, ch).wait_send()
+
+        if d:
+            link(mixed_ref, recv_m.at[d], m_send.at[d], m_recv.at[d], me, ch).wait_send()
     all_sent(send_v, 0)
     all_sent(send_k, 1)
     all_sent(send_c, 2)
-
-
-def long_conv(values, gate, skip, spectrum):
+    pair_w.wait_send()
+    for step in (1, 2, 3, 4):
+        for way in range(2):
+            ring(step, way).wait_send()
+
+
+def block(values, gate, skip, spectrum, weight):
     consts = [jnp.asarray(t) for t in tables()]
-    arrays = [values, gate, skip.reshape(1, -1), spectrum] + consts
+    arrays = [values, gate, skip.reshape(1, -1), spectrum, weight] + consts
     vmem = lambda t: pltpu.VMEM(t.shape, t.dtype)
     held = [vmem(a) for a in arrays[:3]] + [pltpu.VMEM((8, 2, 2, 128, 128), F32)]
     held += [vmem(t) for t in consts]
     dma = pltpu.SemaphoreType.DMA
     return pl.pallas_call(
-        conv_kernel,
-        out_shape=jax.ShapeDtypeStruct(values.shape, BF),
-        in_specs=[pl.BlockSpec(memory_space=pl.ANY)] * len(arrays),
+        block_kernel,
+        out_shape=jax.ShapeDtypeStruct((128, 512), BF),
+        in_specs=[pl.BlockSpec(memory_space=pltpu.HBM)] * len(arrays),
         out_specs=pl.BlockSpec(memory_space=pltpu.VMEM),
         scratch_shapes=held
         + [pltpu.VMEM((SEQ, 16, 128), BF)] * 2
@@ -367,23 +494,26 @@
         + [pltpu.VMEM((SEQ * 16, 128), F32)]
         + [pltpu.VMEM((GRP * 32, 128), F32)] * 2
         + [pltpu.VMEM((GRP * 16, 256), F32)] * 2
-        + [dma((9,)), dma((8,)), dma((3,)), dma((3,)), dma((3,))],
+        + [
+            pltpu.VMEM((2, 8, 64, 1024), BF),
+            pltpu.VMEM((128, 1024), BF),
+            pltpu.VMEM((4, 128, 1024), BF),
+            pltpu.VMEM((4, 128, 512), BF),
+            pltpu.VMEM((4, 128, 512), BF),
+            pltpu.VMEM((4, 128, 512), F32),
+            pltpu.VMEM((5, 128, 512), BF),
+            pltpu.VMEM((4, 128, 512), BF),
+            pltpu.VMEM((128, 512), F32),
+        ]
+        + [dma((9,)), dma((8,)), dma((4,)), dma((3,)), dma((3,))]
+        + [dma((2, 5))] * 2
+        + [dma((4,))] * 6
+        + [dma((2,))],
         compiler_params=pltpu.CompilerParams(
-            collective_id=0, has_side_effects=True, vmem_limit_bytes=40 * 2**20
+            collective_id=0, has_side_effects=True, vmem_limit_bytes=63 * 2**20
         ),
-        name="long_conv",
+        name="hyena_block",
     )(*arrays)
-
-
-def body(values, gate, skip, spectrum, out_weight):
-    mixed = long_conv(values, gate, skip, spectrum)
-    partial_out = lax.dot_general(
-        mixed,
-        lax.all_gather(out_weight, "seq", axis=0, tiled=True),
-        (((1,), (1,)), ((), ())),
-        preferred_element_type=F32,
-    )
-    return lax.psum_scatter(partial_out, "chan", scatter_dimension=1, tiled=True).astype(BF)
 
 
 def solution(mesh):
@@ -395,5 +525,5 @@
         P("seq", "chan"),
     )
     return jax.shard_map(
-        body, mesh=mesh, in_specs=placed, out_specs=P("seq", "chan"), check_vma=False
+        block, mesh=mesh, in_specs=placed, out_specs=P("seq", "chan"), check_vma=False
     )

time: 287 us -> 116 us (0.40)
  the two profiles are of different devices: /device:TPU:6 before, /device:TPU:3 now
where the time goes in v3:
time: 116 us
  Pallas kernels  114 us (98%)
  local copies, waits for them, and re-layouts  1.57 us (1%)
    pallas_call x1, Pallas kernels, block(): pl.pallas_call(block_kernel, out_shape=jax.ShapeDtypeStruct((128, 512), B...  114 us

profile of v3, /device:TPU:3, one launch (start us, length us, event | category | flops | bytes accessed | tf_op | source)
XLA Modules:
  0.0 115.8 jit_solution(9341782275251844742)
XLA Ops:
  0.0 114.2 %hyena_block.1 = bf16[128,512]{1,0:T(8,128)(2,1)} custom-call(bf16[128,1024]{1,0:T(8,128)(2,1)} %values_hbm.1, bf16[128,1024]{1,0:T(8,128)(2,1)} %gate_hbm.1, f32[1,1024]{1,0:T(1,128)} %bitcast.1, f32[2,2,128,1024]{3,2,1,0:T(8,128)} %spec_hbm.1, bf16[64,1024]{1,0:T(8,128)(2,1)} %weight_hbm.1, bf16[144,128]{1,0:T(8,128)(2,1)} %constant.12.clone.ahead_hbm, ...), custom_call_target="tpu_custom_call" | custom-call | tf_op jit(solution)/shard_map/hyena_block/pallas_call | solution.py:485
  114.2 1.6 %copy.13 = bf16[128,512]{1,0:T(8,128)(2,1)} copy(bf16[128,512]{1,0:T(8,128)(2,1)} %hyena_block.1) | data formatting | bytes 262144

commit v4 on v3

--- a/solution.py
+++ b/solution.py
@@ -105,10 +105,10 @@
     values_ref, gate_ref, skip_ref, spec_ref,
     ahead_ref, back_ref, twist_ref, lane_ahead_ref, lane_back_ref, small_ref,
     send_v, recv_v, send_k, recv_k, send_c, recv_c,
-    time_ref, low_ref, high_ref, first_ref, second_ref,
-    w_ref, mixed_ref, recv_m, half_send, half_recv, own_half, z_send, z_recv, done,
+    time_ref, filter_ref, first_ref, second_ref,
+    w_ref, mixed_ref, recv_m, half_send, half_recv, own_half, z_send, z_recv, done, ordered, final,
     in_sem, spec_sem, own_sem, send_sem, recv_sem,
-    ring_send, ring_recv, m_send, m_recv, h_send, h_recv, zs_sem, zr_sem, o_sem,
+    ring_send, ring_recv, m_send, m_recv, h_send, h_recv, zs_sem, zr_sem, o_sem, c_recv, k_recv,
 ):
     me, ch = lax.axis_index("seq"), lax.axis_index("chan")
     x, z, y = me // 16, (me // 8) % 2, me % 8
@@ -116,17 +116,18 @@
     zl, core = ch // 2, ch % 2
     cross = x != zl
 
-    def other(dx, dz, dy):
-        zt = z + dz - 2 * z * dz
-        return wrap(x + dx, 4) * 16 + zt * 8 + wrap(y + dy, 8)
+    xs = [wrap(x + d, 4) * 16 for d in range(4)]
+    zs = [z * 8, 8 - z * 8]
+    ys = [wrap(y + d, 8) for d in range(8)]
+    partners = [
+        xs[dx] + zs[dz] + ys[dy]
+        for dx in range(4) for half in range(2) for dy in range(8)
+        for dz in ((half + dy) % 2,) if dx or dz or dy
+    ]
 
     def each_partner(fn):
-        def step(i, carry):
-            dx, dz, dy = i // 16, (i // 8) % 2, i % 8
-            fn(other(dx, dz, dy))
-            return carry
-
-        lax.fori_loop(1, SEQ, step, 0)
+        for t in partners:
+            fn(t)
 
     loads = []
     for at, (src, dst) in enumerate((
@@ -171,9 +172,10 @@
     def lanes(lt):
         return pl.ds(pl.multiple_of(128 * lt, 128), 128)
 
-    def remote(src, dst, t, at):
+    def remote(src, dst, t, at, here=None):
         return pltpu.make_async_remote_copy(
-            src_ref=src, dst_ref=dst, send_sem=send_sem.at[at], recv_sem=recv_sem.at[at],
+            src_ref=src, dst_ref=dst, send_sem=send_sem.at[at],
+            recv_sem=recv_sem.at[at] if here is None else here,
             device_id={"seq": t}, device_id_type=MESH,
         )
 
@@ -185,22 +187,23 @@
 
     loads[0].wait()
 
-    def pack_values(lt, carry):
-        tiles = swap_lanes(
-            [values_ref[16 * i : 16 * i + 16, lanes(lt)].astype(F32) for i in range(8)]
-        )
-        for d in range(8):
-            send_v[lt * 8 + d] = tiles[d].astype(BF)
+    def pack_values(pair, carry):
+        for lt in (2 * pair, 2 * pair + 1):
+            tiles = swap_lanes(
+                [values_ref[16 * i : 16 * i + 16, lanes(lt)].astype(F32) for i in range(8)]
+            )
+            for d in range(8):
+                send_v[lt * 8 + d] = tiles[d].astype(BF)
         return carry
 
-    lax.fori_loop(0, 8, pack_values, 0)
+    lax.fori_loop(0, 4, pack_values, 0)
     own_v = pltpu.make_async_copy(send_v.at[me], recv_v.at[me], own_sem.at[0])
     own_v.start()
     pl.semaphore_wait(bar, jnp.where(cross, SEQ + 4, SEQ + 3))
-    own_w = pltpu.make_async_copy(weight_hbm, w_ref.at[z, y], own_sem.at[3])
+    own_w = pltpu.make_async_copy(weight_hbm, w_ref.at[z, 0], own_sem.at[3])
     own_w.start()
     pair_w = link(
-        weight_hbm, w_ref.at[z, y], ring_send.at[0, 0], ring_recv.at[0, 0],
+        weight_hbm, w_ref.at[z, 0], ring_send.at[0, 0], ring_recv.at[0, 0],
         x * 16 + (1 - z) * 8 + y, ch,
     )
     pair_w.start()
@@ -211,48 +214,48 @@
     for load in spec_loads:
         load.wait()
 
-    def pack_spectrum(i, carry):
-        dx, dz = i // 2, i % 2
-        lt = wrap(x + dx, 4) * 2 + z + dz - 2 * z * dz
-
-        def plane(q, inner):
-            gl, part = q // 2, q % 2
-            source = jnp.where(upper, 1 - gl, gl)
-            tiles = swap_lanes([
-                spec_ref[lt, part, source, pl.ds(jnp.where(upper, 7 - h, h), 16, stride=8), :]
-                for h in range(8)
-            ])
-            for d in range(8):
-                send_k[lt * 8 + d, pl.ds(pl.multiple_of(16 * q, 16), 16), :] = tiles[d].astype(BF)
-            return inner
-
-        lax.fori_loop(0, 4, plane, 0)
-
-        @pl.when(i > 0)
-        def _():
-            t = lt * 8 + y
-            remote(send_k.at[t], recv_k.at[slot], t, 1).start()
-
-        def to_row(dy, inner):
-            t = lt * 8 + wrap(y + dy, 8)
-            remote(send_k.at[t], recv_k.at[slot], t, 1).start()
-            return inner
-
-        lax.fori_loop(1, 8, to_row, 0)
+    def pack_spectrum(dx, carry):
+        column = wrap(x + dx, 4) * 16
+        for dz in range(2):
+            lt = wrap(x + dx, 4) * 2 + z + dz - 2 * z * dz
+            for q in range(4):
+                gl, part = q // 2, q % 2
+                source = jnp.where(upper, 1 - gl, gl)
+                tiles = swap_lanes([
+                    spec_ref[lt, part, source, pl.ds(jnp.where(upper, 7 - h, h), 16, stride=8), :]
+                    for h in range(8)
+                ])
+                for d in range(8):
+                    send_k[lt * 8 + d, 16 * q : 16 * q + 16, :] = tiles[d].astype(BF)
+
+        def send(dz, dy):
+            t = column + zs[dz] + ys[dy]
+            remote(send_k.at[t], recv_k.at[slot], t, 1, k_recv.at[x * 2 + z]).start()
+
+        for half in range(2):
+            for dy in range(8):
+                dz = (half + dy) % 2
+                if dz or dy:
+                    send(dz, dy)
+                else:
+                    pl.when(dx > 0)(functools.partial(send, dz, dy))
         return carry
 
-    lax.fori_loop(0, 8, pack_spectrum, 0)
+    lax.fori_loop(0, 4, pack_spectrum, 0)
     own_k = pltpu.make_async_copy(send_k.at[me], recv_k.at[slot], own_sem.at[1])
     own_k.start()
     for load in loads[1:]:
         load.wait()
 
     def ring(step, way):
-        at = wrap(y + (9 - step if way == 0 else step - 1), 8)
-        block = w_ref.at[:, at] if step < 4 else w_ref.at[way, at]
+        src = max(0, 2 * step - 3 + way) if step > 1 else 0
+        dst = min(7, 2 * step - 1 + way)
+        here, there = w_ref.at[:, src], w_ref.at[:, dst]
+        if step == 4:
+            here, there = w_ref.at[way, src], w_ref.at[way, dst]
         to = wrap(y + (1 if way == 0 else 7), 8)
         return link(
-            block, block, ring_send.at[way, step], ring_recv.at[way, step], x * 16 + z * 8 + to, ch
+            here, there, ring_send.at[way, step], ring_recv.at[way, step], x * 16 + z * 8 + to, ch
         )
 
     def ring_step(step):
@@ -265,24 +268,23 @@
     all_here(recv_v, 0)
     own_w.wait()
     pair_w.wait_recv()
-    ring_step(1)
     time_ref[...] = recv_v[...].reshape(SEQ * 16, 128).astype(F32)
 
     def over_a(jj, carry):
-        pair = jnp.concatenate(
-            [time_ref[pl.ds(2 * jj + b, SEQ, stride=16), :].astype(BF) for b in range(2)], axis=1
-        )
-        both = jnp.concatenate([pair, pair], axis=0)
+        quad = jnp.concatenate(
+            [time_ref[pl.ds(4 * jj + b, SEQ, stride=16), :].astype(BF) for b in range(4)], axis=1
+        )
+        both = jnp.concatenate([quad, quad], axis=0)
         got = jnp.dot(ahead_ref[...], both, preferred_element_type=F32)
-        for b in range(2):
+        for b in range(4):
             re, im = got[:GRP, 128 * b : 128 * b + 128], got[GRP:, 128 * b : 128 * b + 128]
-            tr, ti = twist_ref[2 * jj + b, 0], twist_ref[2 * jj + b, 1]
-            rows = pl.ds(pl.multiple_of((2 * jj + b) * GRP, 8), GRP)
+            tr, ti = twist_ref[4 * jj + b, 0], twist_ref[4 * jj + b, 1]
+            rows = pl.ds(pl.multiple_of((4 * jj + b) * GRP, 8), GRP)
             first_ref[rows, 0:128] = re * tr - im * ti
             first_ref[rows, 128:256] = re * ti + im * tr
         return carry
 
-    lax.fori_loop(0, 8, over_a, 0)
+    lax.fori_loop(0, 4, over_a, 0)
 
     def over_lanes(src, table, dst):
         def step(b, carry):
@@ -298,21 +300,33 @@
     over_lanes(first_ref, lane_ahead_ref, second_ref)
 
     own_k.wait()
-    all_here(recv_k, 1)
-    ring_step(2)
-    low_ref[pl.ds(64 * 32, 8 * 32), :] = jnp.zeros((8 * 32, 128), F32)
-    high_ref[pl.ds(0, 32), :] = jnp.zeros((32, 128), F32)
-    high_ref[pl.ds(65 * 32, 7 * 32), :] = jnp.zeros((7 * 32, 128), F32)
-
-    def widen(b, carry):
-        rows = pl.multiple_of(b * 256, 32)
-        low_ref[pl.ds(rows, 256), :] = recv_k[pl.ds(4 * b, 4)].reshape(256, 128).astype(F32)
-        high_ref[pl.ds(32 + rows, 256), :] = (
-            recv_k[pl.ds(32 + 4 * b, 4)].reshape(256, 128).astype(F32)
-        )
-        return carry
-
-    lax.fori_loop(0, 8, widen, 0)
+    base = GRP * 32
+    filter_ref[pl.ds(64 * 32, 9 * 32), :] = jnp.zeros((9 * 32, 128), F32)
+    filter_ref[pl.ds(base + 65 * 32, 7 * 32), :] = jnp.zeros((7 * 32, 128), F32)
+
+    def row_here(buf, row, at, sems, own):
+        def wait(count):
+            part = buf.at[pl.ds(row * 8, count)]
+            remote(part, part, me, at, sems.at[row]).wait_recv()
+
+        if own:
+            wait(7)
+        else:
+            wait(8)
+
+    def row_of(dx, dz):
+        return wrap(x + (4 - dx) % 4, 4) * 2 + z + dz - 2 * z * dz
+
+    for dx in range(4):
+        for dz in range(2):
+            row = row_of(dx, dz)
+            row_here(recv_k, row, 1, k_recv, dx + dz == 0)
+            first_slot = jnp.where(row < 4, row * 8, 88 - row * 8)
+            to = first_slot * 64 + jnp.where(row < 4, 0, base + 32 - 32 * 64)
+            filter_ref[pl.ds(pl.multiple_of(to, 32), 512), :] = (
+                recv_k[pl.ds(first_slot, 8)].reshape(512, 128).astype(F32)
+            )
+    ring_step(1)
 
     def filtered(b, carry):
         g = b * 8
@@ -332,12 +346,12 @@
         for h in range(16):
             re, im = freq[h]
             kr = (
-                low_ref[pl.ds(g * 32 + h, 8, stride=32), :]
-                + high_ref[pl.ds(g * 32 + 15 - h, 8, stride=32), :]
+                filter_ref[pl.ds(g * 32 + h, 8, stride=32), :]
+                + filter_ref[pl.ds(base + g * 32 + 15 - h, 8, stride=32), :]
             )
             ki = (
-                low_ref[pl.ds(g * 32 + 16 + h, 8, stride=32), :]
-                - high_ref[pl.ds(g * 32 + 31 - h, 8, stride=32), :]
+                filter_ref[pl.ds(g * 32 + 16 + h, 8, stride=32), :]
+                - filter_ref[pl.ds(base + g * 32 + 31 - h, 8, stride=32), :]
             )
             prod.append((re * kr - im * ki, re * ki + im * kr))
         spread = fft(prod, 1)
@@ -355,117 +369,165 @@
 
     def back_over_a(jj, carry):
         sides = []
-        for b in range(2):
-            rows = pl.ds(pl.multiple_of((2 * jj + b) * GRP, 8), GRP)
+        for b in range(4):
+            rows = pl.ds(pl.multiple_of((4 * jj + b) * GRP, 8), GRP)
             re, im = second_ref[rows, 0:128], second_ref[rows, 128:256]
-            tr, ti = twist_ref[2 * jj + b, 0], twist_ref[2 * jj + b, 1]
+            tr, ti = twist_ref[4 * jj + b, 0], twist_ref[4 * jj + b, 1]
             sides.append(jnp.concatenate([re * tr + im * ti, im * tr - re * ti], axis=0))
         top, low = split(jnp.concatenate(sides, axis=1))
         got = jnp.dot(
             back_ref[...], jnp.concatenate([top, low, top], axis=0), preferred_element_type=F32
         )
-        for b in range(2):
-            time_ref[pl.ds(2 * jj + b, SEQ, stride=16), :] = got[:, 128 * b : 128 * b + 128]
+        for b in range(4):
+            time_ref[pl.ds(4 * jj + b, SEQ, stride=16), :] = got[:, 128 * b : 128 * b + 128]
         return carry
 
-    lax.fori_loop(0, 8, back_over_a, 0)
+    lax.fori_loop(0, 4, back_over_a, 0)
     send_c[...] = time_ref[...].astype(BF).reshape(SEQ, 16, 128)
     own_c = pltpu.make_async_copy(send_c.at[me], recv_c.at[me], own_sem.at[2])
     own_c.start()
-    each_partner(lambda t: remote(send_c.at[t], recv_c.at[me], t, 2).start())
+    each_partner(
+        lambda t: remote(send_c.at[t], recv_c.at[me], t, 2, c_recv.at[x * 2 + z]).start()
+    )
+    ring_step(2)
+    own_c.wait()
+
+    for dx in range(4):
+        for dz in range(2):
+            row_here(recv_c, row_of(dx, dz), 2, c_recv, dx + dz == 0)
+
+        for dz in range(2):
+            lt = row_of(dx, dz)
+            tiles = swap_lanes([recv_c[lt * 8 + d].astype(F32) for d in range(8)])
+            scale = skip_ref[0:1, lanes(lt)]
+            for i in range(8):
+                rows = slice(16 * i, 16 * i + 16)
+                held = values_ref[rows, lanes(lt)].astype(F32)
+                mixed_ref[rows, lanes(lt)] = (
+                    gate_ref[rows, lanes(lt)].astype(F32) * (tiles[i] + scale * held)
+                ).astype(BF)
+
+    def mixed_copy(d):
+        if d % 2:
+            src, dst = mixed_ref, recv_m.at[d]
+        else:
+            rows = pl.ds(0 if d == 2 else 64, 64)
+            src, dst = recv_m.at[1 if d == 2 else 3, rows], recv_m.at[2, rows]
+        to = wrap(x + (1 if d in (1, 2) else 3), 4)
+        return link(src, dst, m_send.at[d], m_recv.at[d], to * 16 + low, ch)
+
+    mixed_copy(1).start()
+    mixed_copy(3).start()
     ring_step(3)
-    own_c.wait()
-    all_here(recv_c, 2)
-    ring_step(4)
-
-    def mix(lt, carry):
-        tiles = swap_lanes([recv_c[lt * 8 + d].astype(F32) for d in range(8)])
-        scale = skip_ref[0:1, lanes(lt)]
-        for i in range(8):
-            rows = slice(16 * i, 16 * i + 16)
-            held = values_ref[rows, lanes(lt)].astype(F32)
-            mixed_ref[rows, lanes(lt)] = (
-                gate_ref[rows, lanes(lt)].astype(F32) * (tiles[i] + scale * held)
-            ).astype(BF)
-        return carry
-
-    lax.fori_loop(0, 8, mix, 0)
-    for d in (1, 3, 2):
-        link(
-            mixed_ref, recv_m.at[d], m_send.at[d], m_recv.at[d], wrap(x + d, 4) * 16 + low, ch
-        ).start()
-    for way in range(2):
-        ring(4, way).wait_recv()
-    order = (0, 1, 3, 2)
-
-    def half_copy(d):
+
+    spans = ((0, 5), (5, 8))
+
+    def rows_of(part):
+        return pl.ds(spans[part][0] * 64, (spans[part][1] - spans[part][0]) * 64)
+
+    def half_copy(d, part):
+        rows = rows_of(part)
         return link(
-            half_send.at[d], half_recv.at[d], h_send.at[d], h_recv.at[d], me, zl * 2 + 1 - core
-        )
-
-    def multiply(d):
-        src = mixed_ref
-        if d:
-            link(mixed_ref, recv_m.at[d], m_send.at[d], m_recv.at[d], me, ch).wait_recv()
-            src = recv_m.at[d]
+            half_send.at[d, rows], half_recv.at[d, rows], h_send.at[part, d], h_recv.at[part, d],
+            me, zl * 2 + 1 - core,
+        )
+
+    def multiply(d, part):
+        src = recv_m.at[d] if d else mixed_ref
+        first, last = spans[part]
+        rows = rows_of(part)
         for side in range(2):
             half = 1 - core if side == 0 else core
             got = lax.dot_general(
-                src[...], w_ref[half].reshape(512, 1024), (((1,), (1,)), ((), ())),
-                preferred_element_type=F32,
+                w_ref[half, first:last].reshape((last - first) * 64, 1024), src[...],
+                (((1,), (1,)), ((), ())), preferred_element_type=F32,
             )
             if side == 0:
-                half_send[d] = got.astype(BF)
-                half_copy(d).start()
+                half_send[d, rows] = got.astype(BF)
+                half_copy(d, part).start()
             else:
-                own_half[d] = got
-
-    def pass_on(d):
-        half_copy(d).wait_recv()
+                own_half[d, rows] = got
+
+    def z_copy(d, part, target):
+        rows = rows_of(part)
+        return link(
+            z_send.at[d, rows], z_recv.at[zl, rows], zs_sem.at[part, d], zr_sem.at[part, zl],
+            me, target * 2 + core,
+        )
+
+    def pass_on(d, part):
+        half_copy(d, part).wait_recv()
         target = wrap(x + 4 - d, 4)
-        total = own_half[d] + half_recv[d].astype(F32)
+        rows = rows_of(part)
+        total = own_half[d, rows] + half_recv[d, rows].astype(F32)
 
         @pl.when(target == zl)
         def _():
-            done[...] = total
+            done[rows, :] = total
 
         @pl.when(target != zl)
         def _():
-            z_send[d] = total.astype(BF)
+            z_send[d, rows] = total.astype(BF)
+            z_copy(d, part, target).start()
+
+    multiply(0, 0)
+    pass_on(0, 0)
+    ring_step(4)
+    mixed_copy(1).wait_recv()
+    mixed_copy(2).start()
+    mixed_copy(3).wait_recv()
+    mixed_copy(0).start()
+    multiply(1, 0)
+    multiply(3, 0)
+    pass_on(1, 0)
+    pass_on(3, 0)
+    for way in range(2):
+        ring(4, way).wait_recv()
+    multiply(0, 1)
+    multiply(1, 1)
+    multiply(3, 1)
+    pass_on(0, 1)
+    pass_on(1, 1)
+    pass_on(3, 1)
+    mixed_copy(2).wait_recv()
+    mixed_copy(0).wait_recv()
+    multiply(2, 0)
+    multiply(2, 1)
+    pass_on(2, 0)
+    pass_on(2, 1)
+    for part in range(2):
+        rows = rows_of(part)
+        for d in (1, 2, 3):
+            peer = wrap(zl + d, 4)
             link(
-                z_send.at[d], z_recv.at[zl], zs_sem.at[d], zr_sem.at[zl], me, target * 2 + core
-            ).start()
-
-    for at, d in enumerate(order):
-        multiply(d)
-        if at:
-            pass_on(order[at - 1])
-    pass_on(order[-1])
-    for d in (1, 2, 3):
-        peer = wrap(zl + d, 4)
-        link(z_send.at[0], z_recv.at[peer], zs_sem.at[0], zr_sem.at[peer], me, ch).wait_recv()
-        done[...] += z_recv[peer].astype(F32)
+                z_send.at[0, rows], z_recv.at[peer, rows], zs_sem.at[part, 0],
+                zr_sem.at[part, peer], me, ch,
+            ).wait_recv()
+            done[rows, :] += z_recv[peer, rows].astype(F32)
+    for slot_at, dy in enumerate((0, 7, 1, 6, 2, 5, 3, 4)):
+        to = pl.multiple_of(wrap(y + dy, 8) * 64, 64)
+        ordered[pl.ds(to, 64), :] = done[slot_at * 64 : slot_at * 64 + 64, :]
 
     @pl.when(cross)
     def _():
-        z_send[4] = done[...].astype(BF)
-        last = link(z_send.at[4], out_ref, o_sem.at[0], o_sem.at[1], zl * 16 + low, x * 2 + core)
+        final[...] = ordered[...].T.astype(BF)
+        last = link(final, out_ref, o_sem.at[0], o_sem.at[1], zl * 16 + low, x * 2 + core)
         last.start()
         last.wait()
 
     @pl.when(jnp.logical_not(cross))
     def _():
-        out_ref[...] = done[...].astype(BF)
+        out_ref[...] = ordered[...].T.astype(BF)
 
     for d in range(4):
-        half_copy(d).wait_send()
-
-        @pl.when(wrap(x + 4 - d, 4) != zl)
-        def _(d=d):
-            link(z_send.at[d], z_recv.at[0], zs_sem.at[d], zr_sem.at[0], me, ch).wait_send()
-
-        if d:
-            link(mixed_ref, recv_m.at[d], m_send.at[d], m_recv.at[d], me, ch).wait_send()
+        mixed_copy(d).wait_send()
+        for part in range(2):
+            half_copy(d, part).wait_send()
+
+            @pl.when(wrap(x + 4 - d, 4) != zl)
+            def _(d=d, part=part):
+                z_copy(d, part, zl).wait_send()
+
     all_sent(send_v, 0)
     all_sent(send_k, 1)
     all_sent(send_c, 2)
@@ -492,23 +554,26 @@
         + [pltpu.VMEM((SEQ, 64, 128), BF)] * 2
         + [pltpu.VMEM((SEQ, 16, 128), BF)] * 2
         + [pltpu.VMEM((SEQ * 16, 128), F32)]
-        + [pltpu.VMEM((GRP * 32, 128), F32)] * 2
+        + [pltpu.VMEM((2 * GRP * 32, 128), F32)]
         + [pltpu.VMEM((GRP * 16, 256), F32)] * 2
         + [
             pltpu.VMEM((2, 8, 64, 1024), BF),
             pltpu.VMEM((128, 1024), BF),
             pltpu.VMEM((4, 128, 1024), BF),
-            pltpu.VMEM((4, 128, 512), BF),
-            pltpu.VMEM((4, 128, 512), BF),
-            pltpu.VMEM((4, 128, 512), F32),
-            pltpu.VMEM((5, 128, 512), BF),
-            pltpu.VMEM((4, 128, 512), BF),
-            pltpu.VMEM((128, 512), F32),
+            pltpu.VMEM((4, 512, 128), BF),
+            pltpu.VMEM((4, 512, 128), BF),
+            pltpu.VMEM((4, 512, 128), F32),
+            pltpu.VMEM((4, 512, 128), BF),
+            pltpu.VMEM((4, 512, 128), BF),
+            pltpu.VMEM((512, 128), F32),
+            pltpu.VMEM((512, 128), F32),
+            pltpu.VMEM((128, 512), BF),
         ]
         + [dma((9,)), dma((8,)), dma((4,)), dma((3,)), dma((3,))]
         + [dma((2, 5))] * 2
-        + [dma((4,))] * 6
-        + [dma((2,))],
+        + [dma((4,))] * 2
+        + [dma((2, 4))] * 4
+        + [dma((2,)), dma((8,)), dma((8,))],
         compiler_params=pltpu.CompilerParams(
             collective_id=0, has_side_effects=True, vmem_limit_bytes=63 * 2**20
         ),

time: 116 us -> 108 us (0.931)
  Pallas kernels: 114 us -> 106 us
    pallas_call x1, Pallas kernels: 114 us -> 106 us  [block(): pl.pallas_call(block_kernel, out_shape=jax.ShapeDtypeStruct((128, 512), B...]
where the time goes in v4:
time: 108 us
  Pallas kernels  106 us (98%)
  local copies, waits for them, and re-layouts  1.57 us (1%)
    pallas_call x1, Pallas kernels, block(): pl.pallas_call(block_kernel, out_shape=jax.ShapeDtypeStruct((128, 512), B...  106 us

profile of v4, /device:TPU:3, one launch (start us, length us, event | category | flops | bytes accessed | tf_op | source)
XLA Modules:
  0.0 107.5 jit_solution(1450244073157639422)
XLA Ops:
  0.0 106.0 %hyena_block.1 = bf16[128,512]{1,0:T(8,128)(2,1)} custom-call(bf16[128,1024]{1,0:T(8,128)(2,1)} %values_hbm.1, bf16[128,1024]{1,0:T(8,128)(2,1)} %gate_hbm.1, f32[1,1024]{1,0:T(1,128)} %bitcast.1, f32[2,2,128,1024]{3,2,1,0:T(8,128)} %spec_hbm.1, bf16[64,1024]{1,0:T(8,128)(2,1)} %weight_hbm.1, bf16[144,128]{1,0:T(8,128)(2,1)} %constant.12.clone.ahead_hbm, ...), custom_call_target="tpu_custom_call" | custom-call | tf_op jit(solution)/shard_map/hyena_block/pallas_call | solution.py:547
  106.0 1.6 %copy.13 = bf16[128,512]{1,0:T(8,128)(2,1)} copy(bf16[128,512]{1,0:T(8,128)(2,1)} %hyena_block.1) | data formatting | bytes 262144

commit v5 on v4

--- a/solution.py
+++ b/solution.py
@@ -114,7 +114,7 @@
     x, z, y = me // 16, (me // 8) % 2, me % 8
     low = me % 16
     zl, core = ch // 2, ch % 2
-    cross = x != zl
+    cross = x + zl > 0
 
     xs = [wrap(x + d, 4) * 16 for d in range(4)]
     zs = [z * 8, 8 - z * 8]
@@ -161,7 +161,7 @@
 
     @pl.when(cross)
     def _():
-        greet(zl * 16 + low, x * 2 + core)
+        greet(zl * 16 + low, wrap(zl + 4 - x, 4) * 2 + core)
 
     def link(src, dst, ss, rs, seq, chan):
         return pltpu.make_async_remote_copy(
@@ -392,6 +392,17 @@
     ring_step(2)
     own_c.wait()
 
+    def mixed_copy(d, columns=None):
+        if d % 2:
+            src, dst = mixed_ref, recv_m.at[d]
+            if columns is not None:
+                src, dst = src.at[:, columns], dst.at[:, columns]
+        else:
+            rows = pl.ds(0 if d == 2 else 64, 64)
+            src, dst = recv_m.at[1 if d == 2 else 3, rows], recv_m.at[2, rows]
+        to = wrap(x + (1 if d in (1, 2) else 3), 4)
+        return link(src, dst, m_send.at[d], m_recv.at[d], to * 16 + low, ch)
+
     for dx in range(4):
         for dz in range(2):
             row_here(recv_c, row_of(dx, dz), 2, c_recv, dx + dz == 0)
@@ -406,19 +417,12 @@
                 mixed_ref[rows, lanes(lt)] = (
                     gate_ref[rows, lanes(lt)].astype(F32) * (tiles[i] + scale * held)
                 ).astype(BF)
-
-    def mixed_copy(d):
-        if d % 2:
-            src, dst = mixed_ref, recv_m.at[d]
-        else:
-            rows = pl.ds(0 if d == 2 else 64, 64)
-            src, dst = recv_m.at[1 if d == 2 else 3, rows], recv_m.at[2, rows]
-        to = wrap(x + (1 if d in (1, 2) else 3), 4)
-        return link(src, dst, m_send.at[d], m_recv.at[d], to * 16 + low, ch)
-
-    mixed_copy(1).start()
-    mixed_copy(3).start()
-    ring_step(3)
+        columns = pl.ds(pl.multiple_of(wrap(x + (4 - dx) % 4, 4) * 256, 256), 256)
+        mixed_copy(1, columns).start()
+        mixed_copy(3, columns).start()
+        if dx == 2:
+            ring_step(3)
+
 
     spans = ((0, 5), (5, 8))
 
@@ -448,27 +452,26 @@
             else:
                 own_half[d, rows] = got
 
-    def z_copy(d, part, target):
+    def z_copy(d, part):
         rows = rows_of(part)
         return link(
             z_send.at[d, rows], z_recv.at[zl, rows], zs_sem.at[part, d], zr_sem.at[part, zl],
-            me, target * 2 + core,
+            me, 2 * d + core,
         )
 
     def pass_on(d, part):
         half_copy(d, part).wait_recv()
-        target = wrap(x + 4 - d, 4)
         rows = rows_of(part)
         total = own_half[d, rows] + half_recv[d, rows].astype(F32)
 
-        @pl.when(target == zl)
+        @pl.when(zl == d)
         def _():
             done[rows, :] = total
 
-        @pl.when(target != zl)
+        @pl.when(zl != d)
         def _():
             z_send[d, rows] = total.astype(BF)
-            z_copy(d, part, target).start()
+            z_copy(d, part).start()
 
     multiply(0, 0)
     pass_on(0, 0)
@@ -511,7 +514,8 @@
     @pl.when(cross)
     def _():
         final[...] = ordered[...].T.astype(BF)
-        last = link(final, out_ref, o_sem.at[0], o_sem.at[1], zl * 16 + low, x * 2 + core)
+        to = wrap(x + 4 - zl, 4) * 16 + low
+        last = link(final, out_ref, o_sem.at[0], o_sem.at[1], to, x * 2 + core)
         last.start()
         last.wait()
 
@@ -524,9 +528,9 @@
         for part in range(2):
             half_copy(d, part).wait_send()
 
-            @pl.when(wrap(x + 4 - d, 4) != zl)
+            @pl.when(zl != d)
             def _(d=d, part=part):
-                z_copy(d, part, zl).wait_send()
+                z_copy(d, part).wait_send()
 
     all_sent(send_v, 0)
     all_sent(send_k, 1)

time: 108 us -> 107 us (level)
  the two profiles are of different devices: /device:TPU:3 before, /device:TPU:6 now
where the time goes in v5:
time: 107 us
  Pallas kernels  105 us (98%)
  local copies, waits for them, and re-layouts  1.57 us (1%)
    pallas_call x1, Pallas kernels, block(): pl.pallas_call(block_kernel, out_shape=jax.ShapeDtypeStruct((128, 512), B...  105 us

profile of v5, /device:TPU:6, one launch (start us, length us, event | category | flops | bytes accessed | tf_op | source)
XLA Modules:
  0.0 107.0 jit_solution(16092540787703027805)
XLA Ops:
  0.0 105.4 %hyena_block.1 = bf16[128,512]{1,0:T(8,128)(2,1)} custom-call(bf16[128,1024]{1,0:T(8,128)(2,1)} %values_hbm.1, bf16[128,1024]{1,0:T(8,128)(2,1)} %gate_hbm.1, f32[1,1024]{1,0:T(1,128)} %bitcast.1, f32[2,2,128,1024]{3,2,1,0:T(8,128)} %spec_hbm.1, bf16[64,1024]{1,0:T(8,128)(2,1)} %weight_hbm.1, bf16[144,128]{1,0:T(8,128)(2,1)} %constant.12.clone.ahead_hbm, ...), custom_call_target="tpu_custom_call" | custom-call | tf_op jit(solution)/shard_map/hyena_block/pallas_call | solution.py:551
  105.4 1.6 %copy.13 = bf16[128,512]{1,0:T(8,128)(2,1)} copy(bf16[128,512]{1,0:T(8,128)(2,1)} %hyena_block.1) | data formatting | bytes 262144

commit v6 on v5

--- a/solution.py
+++ b/solution.py
@@ -513,7 +513,7 @@
 
     @pl.when(cross)
     def _():
-        final[...] = ordered[...].T.astype(BF)
+        final[...] = ordered[...].astype(BF)
         to = wrap(x + 4 - zl, 4) * 16 + low
         last = link(final, out_ref, o_sem.at[0], o_sem.at[1], to, x * 2 + core)
         last.start()
@@ -521,7 +521,7 @@
 
     @pl.when(jnp.logical_not(cross))
     def _():
-        out_ref[...] = ordered[...].T.astype(BF)
+        out_ref[...] = ordered[...].astype(BF)
 
     for d in range(4):
         mixed_copy(d).wait_send()
@@ -550,7 +550,7 @@
     dma = pltpu.SemaphoreType.DMA
     return pl.pallas_call(
         block_kernel,
-        out_shape=jax.ShapeDtypeStruct((128, 512), BF),
+        out_shape=jax.ShapeDtypeStruct((512, 128), BF),
         in_specs=[pl.BlockSpec(memory_space=pltpu.HBM)] * len(arrays),
         out_specs=pl.BlockSpec(memory_space=pltpu.VMEM),
         scratch_shapes=held
@@ -571,7 +571,7 @@
             pltpu.VMEM((4, 512, 128), BF),
             pltpu.VMEM((512, 128), F32),
             pltpu.VMEM((512, 128), F32),
-            pltpu.VMEM((128, 512), BF),
+            pltpu.VMEM((512, 128), BF),
         ]
         + [dma((9,)), dma((8,)), dma((4,)), dma((3,)), dma((3,))]
         + [dma((2, 5))] * 2
@@ -582,7 +582,7 @@
             collective_id=0, has_side_effects=True, vmem_limit_bytes=63 * 2**20
         ),
         name="hyena_block",
-    )(*arrays)
+    )(*arrays).T
 
 
 def solution(mesh):

time: 107 us -> 107 us (level)
    transpose x0 -> x1, local copies, waits for them, and re-layouts: none -> 1.67 us  [block(): return pl.pallas_call(block_kernel, out_shape=jax.ShapeDtypeStruct((512,...]
    unnamed x1 -> x0, local copies, waits for them, and re-layouts: 1.57 us -> none
where the time goes in v6:
time: 107 us
  Pallas kernels  105 us (98%)
  local copies, waits for them, and re-layouts  1.67 us (2%)
    pallas_call x1, Pallas kernels, block(): pl.pallas_call(block_kernel, out_shape=jax.ShapeDtypeStruct((512, 128), B...  105 us

profile of v6, /device:TPU:6, one launch (start us, length us, event | category | flops | bytes accessed | tf_op | source)
XLA Modules:
  0.0 107.0 jit_solution(17037746743609150883)
XLA Ops:
  0.0 105.3 %hyena_block.1 = bf16[512,128]{1,0:T(8,128)(2,1)} custom-call(bf16[128,1024]{1,0:T(8,128)(2,1)} %values_hbm.1, bf16[128,1024]{1,0:T(8,128)(2,1)} %gate_hbm.1, f32[1,1024]{1,0:T(1,128)} %bitcast.3, f32[2,2,128,1024]{3,2,1,0:T(8,128)} %spec_hbm.1, bf16[64,1024]{1,0:T(8,128)(2,1)} %weight_hbm.1, bf16[144,128]{1,0:T(8,128)(2,1)} %constant.12.clone.ahead_hbm, ...), custom_call_target="tpu_custom_call" | custom-call | tf_op jit(solution)/shard_map/hyena_block/pallas_call | solution.py:551
  105.4 1.7 %copy.12 = bf16[128,512]{1,0:T(8,128)(2,1)} copy(bf16[128,512]{0,1:T(8,128)(2,1)} %bitcast.2) | data formatting | bytes 262144 | tf_op jit(solution)/shard_map/transpose | solution.py:585
